TPU v7x, 256 devices: a whole 4x4x8 slice. The times are simulated.
256 devices in a mesh: resp: 8 (over y_lo, x), prompt: 32 (over y_hi, z, core).
Axes of the slice: x: 4, y: 4 (y_hi: 2, y_lo: 2; y = y_hi * 2 + y_lo), z: 8, core: 2. Of those that a mesh axis runs over, the one named last changes fastest.
Arguments:
- resp_q: bfloat16 [32, 8, 256, 2560], P('prompt', 'resp'), may hold values from -9 to 9, as said below
- resp_kv: bfloat16 [32, 8, 256, 2, 512], P('prompt', 'resp'), may hold values from -6 to 6
- prompt_kv: bfloat16 [32, 1024, 2, 512], P('prompt', 'resp'), may hold values from -9 to 9
- bias: float32 [512], replicated, may hold values from -3 to 3
- prompt_len: int32 [32], P('prompt'), may hold values from 256 to 1024, as said below
- resp_len: int32 [32, 8], P('prompt', 'resp'), may hold values from 64 to 256, as said below
- d_out: bfloat16 [32, 8, 256, 2560], P('prompt', 'resp'), may hold values from -6 to 6
Outputs:
- attn_out: bfloat16 [32, 8, 256, 2560], P('prompt', 'resp')
- d_q: bfloat16 [32, 8, 256, 2560], P('prompt', 'resp')
- d_resp_kv: bfloat16 [32, 8, 256, 2, 512], P('prompt', 'resp')
- d_prompt_kv: bfloat16 [32, 1024, 2, 512], P('prompt', 'resp')
- d_bias: float32 [512], replicated
Inputs may be any that keep to these rules, and one draw needn't show every extreme that they name: `prompt_len`: tokens of each prompt; some prompt has all 1024 slots filled. `resp_len`: tokens of each response; some response fills all 256 slots. `resp_q`: query entries.
All inputs are finite; a program needn't handle non-finite values.
Results may differ from a plain program's by a relative error of at most 0.024.
Values may be sent and summed in bfloat16 or wider, within the bound.
No kernel may reach another device: no remote copies, remote signals or barrier semaphores. Data moves between devices by JAX's collectives and lax.ppermute only.
A program may use at most 128 MiB of HBM per device.

v0:
```python
import jax
import jax.numpy as jnp
from jax import lax
from jax.sharding import PartitionSpec as P

KVH = 4
HD = 128
GROUP = 5


def member_pass(queries, own_side, prompt_side, prompt_count, resp_count, cotangent):
    row_count = queries.shape[0]
    prompt_total = prompt_side.shape[0]
    scaling = HD ** (-0.5)
    key_table = jnp.concatenate([prompt_side, own_side], axis=0)
    positions = jnp.arange(row_count, dtype=jnp.int32)
    live_rows = positions < resp_count
    prompt_mask = jnp.broadcast_to(
        jnp.arange(prompt_total, dtype=jnp.int32)[None, :] < prompt_count, (row_count, prompt_total)
    )
    causal = positions[None, :] <= positions[:, None]
    allowed = jnp.concatenate([prompt_mask, causal], axis=1)
    head_queries = queries.reshape(row_count, KVH, GROUP, HD)
    d_live = jnp.where(live_rows[:, None], cotangent, jnp.zeros_like(cotangent)).reshape(
        row_count, KVH, GROUP, HD
    )
    out_list, dq_list, grads_k, grads_v = ([], [], [], [])
    for kv_head in range(KVH):
        key_block = key_table[:, 0, kv_head * HD : (kv_head + 1) * HD]
        value_block = key_table[:, 1, kv_head * HD : (kv_head + 1) * HD]
        query_group = head_queries[:, kv_head]
        scores = (
            jnp.einsum("rhd,kd->rhk", query_group, key_block, preferred_element_type=jnp.float32)
            * scaling
        )
        scores = jnp.where(allowed[:, None, :], scores, -jnp.inf)
        row_max = jnp.max(scores, axis=-1, keepdims=True)
        log_total = row_max + jnp.log(jnp.sum(jnp.exp(scores - row_max), axis=-1, keepdims=True))
        weights = jnp.exp(scores - log_total)
        weights_low = weights.astype(jnp.bfloat16)
        combined = jnp.einsum(
            "rhk,kd->rhd", weights_low, value_block, preferred_element_type=jnp.float32
        )
        attended = jnp.where(live_rows[:, None, None], combined, jnp.zeros_like(combined)).astype(
            jnp.bfloat16
        )
        upstream = d_live[:, kv_head]
        row_dot = jnp.sum(
            upstream.astype(jnp.float32) * attended.astype(jnp.float32), axis=-1, keepdims=True
        )
        d_weights = jnp.einsum(
            "rhd,kd->rhk", upstream, value_block, preferred_element_type=jnp.float32
        )
        d_scores = (weights * (d_weights - row_dot) * scaling).astype(jnp.bfloat16)
        d_query = jnp.einsum(
            "rhk,kd->rhd", d_scores, key_block, preferred_element_type=jnp.float32
        ).astype(jnp.bfloat16)
        grads_k.append(
            jnp.einsum("rhk,rhd->kd", d_scores, query_group, preferred_element_type=jnp.float32)
        )
        grads_v.append(
            jnp.einsum("rhk,rhd->kd", weights_low, upstream, preferred_element_type=jnp.float32)
        )
        out_list.append(attended)
        dq_list.append(d_query)
    attended_all = jnp.stack(out_list, axis=1).reshape(row_count, KVH * GROUP * HD)
    d_query_all = jnp.stack(dq_list, axis=1).reshape(row_count, KVH * GROUP * HD)
    column_grad = jnp.stack(
        [jnp.concatenate(grads_k, axis=1), jnp.concatenate(grads_v, axis=1)], axis=1
    )
    resp_grad = column_grad[prompt_total:]
    prompt_low = lax.optimization_barrier(column_grad[:prompt_total].astype(jnp.bfloat16))
    return (
        attended_all,
        d_query_all,
        resp_grad.astype(jnp.bfloat16),
        prompt_low.astype(jnp.float32),
        jnp.sum(resp_grad[:, 1], axis=0),
    )


def with_bias(pairs, bias):
    return jnp.stack(
        [pairs[:, 0].astype(jnp.float32), pairs[:, 1].astype(jnp.float32) + bias], axis=1
    ).astype(jnp.bfloat16)


def shards(resp_q, resp_kv, prompt_kv, bias, prompt_len, resp_len, d_out):
    own_rows = prompt_kv[0]
    row_share = own_rows.shape[0]
    own_side = with_bias(own_rows, bias)
    prompt_side = lax.all_gather(own_side, "resp", axis=0, tiled=True)
    resp_side = with_bias(resp_kv[0, 0], bias)
    attended_all, d_query_all, d_resp_all, prompt_part, value_sums = member_pass(
        resp_q[0, 0], resp_side, prompt_side, prompt_len[0], resp_len[0, 0], d_out[0, 0]
    )
    summed_all = lax.psum(prompt_part.astype(jnp.bfloat16), "resp").astype(jnp.float32)
    owned_rows = lax.dynamic_slice_in_dim(
        summed_all, lax.axis_index("resp") * row_share, row_share, 0
    )
    local_term = value_sums + jnp.sum(owned_rows[:, 1], axis=0)
    bias_total = lax.psum(local_term, ("resp", "prompt"))
    d_bias = bias_total / (lax.axis_size("resp") * lax.axis_size("prompt"))
    return (
        attended_all[None, None],
        d_query_all[None, None],
        d_resp_all[None, None],
        owned_rows.astype(jnp.bfloat16)[None],
        d_bias,
    )


def solution(mesh):
    return jax.shard_map(
        shards,
        mesh=mesh,
        in_specs=(
            P("prompt", "resp", None, None),
            P("prompt", "resp", None, None, None),
            P("prompt", "resp", None, None),
            P(),
            P("prompt"),
            P("prompt", "resp"),
            P("prompt", "resp", None, None),
        ),
        out_specs=(
            P("prompt", "resp", None, None),
            P("prompt", "resp", None, None),
            P("prompt", "resp", None, None, None),
            P("prompt", "resp", None, None),
            P(),
        ),
        check_vma=False,
    )
```

profile of v0, /device:TPU:2, one launch (start us, length us, event | category | flops | bytes accessed | tf_op | source)
XLA Modules:
  0.0 268.6 jit_solution(17350943833187757910)
XLA Ops:
  12.3 1.4 copy.57
  15.2 1.1 broadcast_select_fusion
  16.6 38.5 %all-gather.2.cloned.1.call-done = bf16[1024,2,512]{2,0,1:T(8,128)(2,1)} async-done(((bf16[128,2,512]{2,0,1:T(8,128)(2,1)}), bf16[1024,2,512]{2,0,1:T(8,128)(2,1)}) %all-gather.2.cloned.1.call-update) | async-done | bytes 2097168 | tf_op jit(solution)/shard_map/all_gather | solution.py:92
  55.1 1.9 maximum_maximum_fusion
  57.0 2.2 fusion.24
  61.3 1.2 fusion.7
  62.6 1.2 convolution_bitcast_fusion.1
  64.8 1.2 fusion.6
  66.0 1.2 convolution_bitcast_fusion.2
  70.4 1.4 fusion.8
  71.9 1.3 convolution_bitcast_fusion
  74.0 1.3 convolution_bitcast_fusion.3
  75.3 2.2 multiply_reduce_fusion.3
  77.6 3.3 %multiply_convert_fusion.2 = bf16[256,5,1280]{0,2,1:T(8,128)(2,1)} fusion(f32[256,5,1280]{0,2,1:T(8,128)S(1)} %get-tuple-element.26, f32[256,5]{0,1:T(8,128)S(1)} %get-tuple-element.18, f32[256,5]{0,1:T(8,128)S(1)} %log_add_fusion.2, bf16[1280,2,512]{2,0,1:T(8,128)(2,1)S(1)} %maximum_maximum_fusion, bf16[256,4,5,128]{0,3,2,1:T(8,128)(2,1)S(1)} %copy-done), kind=kOutput, calls=%fused_computation.6 | convolution fusion | flops 427622400 | bytes 10502144 | tf_op jit(solution)/shard_map/rhd,kd->rhk/dot_general | solution.py:51
  80.9 1.7 multiply_convert_fusion.1
  82.6 1.7 multiply_convert_fusion.3
  84.3 1.2 convolution_bitcast_fusion.7
  85.5 1.2 convolution_bitcast_fusion.5
  87.4 1.2 convolution_bitcast_fusion.6
  88.6 1.9 multiply_convert_fusion
  90.5 1.2 convolution_bitcast_fusion.4
  93.7 1.6 fusion.4
  95.4 2.3 pad_maximum_fusion.2
  97.7 2.4 copy.99
  100.1 2.7 %fusion.9 = bf16[256,1,5,128]{0,3,2,1:T(8,128)(2,1)S(1)} fusion(bf16[256,5,1280]{0,2,1:T(8,128)(2,1)} %copy-done.14, bf16[1280,2,512]{2,0,1:T(8,128)(2,1)S(1)} %maximum_maximum_fusion), kind=kOutput, calls=%fused_computation.49 | convolution fusion | flops 419594240 | bytes 3932160 | tf_op jit(solution)/shard_map/rhk,kd->rhd/dot_general | solution.py:55
  102.8 2.7 %fusion.11 = bf16[256,1,5,128]{0,3,2,1:T(8,128)(2,1)S(1)} fusion(bf16[256,5,1280]{0,2,1:T(8,128)(2,1)} %copy-done.13, bf16[1280,2,512]{2,0,1:T(8,128)(2,1)S(1)} %maximum_maximum_fusion), kind=kOutput, calls=%fused_computation.51 | convolution fusion | flops 419594240 | bytes 3932160 | tf_op jit(solution)/shard_map/rhk,kd->rhd/dot_general | solution.py:55
  106.9 1.2 pad_maximum_fusion.3
  108.1 2.6 copy.100
  111.6 2.0 copy.101
  113.6 1.7 pad_maximum_fusion.1
  115.4 68.2 %all-reduce.2.cloned.1.call-done = bf16[1024,2,512]{0,2,1:T(8,128)(2,1)} async-done(((bf16[1024,2,512]{0,2,1:T(8,128)(2,1)}), bf16[1024,2,512]{0,2,1:T(8,128)(2,1)}) %all-reduce.2.cloned.1.call-update) | async-done | bytes 2097168 | tf_op jit(solution)/shard_map/psum | solution.py:97
  184.8 75.6 %psum.15 = f32[512]{0:T(512)S(1)} all-reduce(f32[512]{0:T(512)S(1)} %add.69), channel_id=1, replica_groups=mesh['resp'=8,'prompt'=32] {'resp','prompt'}, use_global_device_ids=true, to_apply=%region_15.16 | all-reduce | flops 512 | bytes 4096 | tf_op jit(solution)/shard_map/psum | solution.py:102
  (84 shorter events, 20.1 us)
Async XLA Ops:
  7.2 5.2 %copy-start.20 = (bf16[1,1,256,2560]{3,2,1,0:T(8,128)(2,1)S(1)}, bf16[1,1,256,2560]{3,2,1,0:T(8,128)(2,1)}, u32[]{:S(2)}) copy-start(bf16[1,1,256,2560]{3,2,1,0:T(8,128)(2,1)} %param.7) | copy-start | bytes 3932164
  7.2 6.6 %copy-start.21 = (bf16[1,1,256,2560]{3,2,1,0:T(8,128)(2,1)S(1)}, bf16[1,1,256,2560]{3,2,1,0:T(8,128)(2,1)}, u32[]{:S(2)}) copy-start(bf16[1,1,256,2560]{3,2,1,0:T(8,128)(2,1)} %param.13) | copy-start | bytes 3932164
  7.2 48.0 %all-gather.2.cloned.1.call-start = ((), (), s32[]{:S(2)}) async-start(), calls=%async_computation | async-start | bytes 2359296 | tf_op jit(solution)/shard_map/all_gather | solution.py:92
  9.8 173.7 %all-reduce.2.cloned.1.call-start = ((), (), s32[]{:S(2)}) async-start(), calls=%async_computation.1 | async-start | bytes 4194304 | tf_op jit(solution)/shard_map/psum | solution.py:97
  11.2 3.3 %copy-start.22 = (f32[512]{0:T(512)S(1)}, f32[512]{0:T(512)}, u32[]{:S(2)}) copy-start(f32[512]{0:T(512)} %param.10) | copy-start | bytes 6148
  57.0 2.2 copy-start.10
  61.3 1.3 copy-start
  63.9 27.9 %copy-start.5 = (f32[1280,128]{0,1:T(8,128)}, f32[1280,128]{0,1:T(8,128)S(1)}, u32[]{:S(2)}) copy-start(f32[1280,128]{0,1:T(8,128)S(1)} %convolution_bitcast_fusion.1) | copy-start | bytes 1966084
  66.0 9.3 %copy-start.17 = (bf16[256,5,128]{0,2,1:T(8,128)(2,1)}, bf16[256,5,128]{0,2,1:T(8,128)(2,1)S(1)}, u32[]{:S(2)}) copy-start(bf16[256,5,128]{0,2,1:T(8,128)(2,1)S(1)} %fusion.6) | copy-start | bytes 983044
  67.3 24.5 %copy-start.7 = (f32[1280,128]{0,1:T(8,128)}, f32[1280,128]{0,1:T(8,128)S(1)}, u32[]{:S(2)}) copy-start(f32[1280,128]{0,1:T(8,128)S(1)} %convolution_bitcast_fusion.2) | copy-start | bytes 1966084
  71.8 3.5 %copy-start.19 = (bf16[256,5,128]{0,2,1:T(8,128)(2,1)}, bf16[256,5,128]{0,2,1:T(8,128)(2,1)S(1)}, u32[]{:S(2)}) copy-start(bf16[256,5,128]{0,2,1:T(8,128)(2,1)S(1)} %fusion.8) | copy-start | bytes 983044
  73.1 18.7 %copy-start.8 = (f32[1280,128]{0,1:T(8,128)}, f32[1280,128]{0,1:T(8,128)S(1)}, u32[]{:S(2)}) copy-start(f32[1280,128]{0,1:T(8,128)S(1)} %convolution_bitcast_fusion) | copy-start | bytes 1966084
  75.3 16.5 %copy-start.9 = (f32[1280,128]{0,1:T(8,128)}, f32[1280,128]{0,1:T(8,128)S(1)}, u32[]{:S(2)}) copy-start(f32[1280,128]{0,1:T(8,128)S(1)} %convolution_bitcast_fusion.3) | copy-start | bytes 1966084
  82.6 2.9 %copy-start.13 = (bf16[256,5,1280]{0,2,1:T(8,128)(2,1)}, bf16[256,5,1280]{0,2,1:T(8,128)(2,1)S(1)}, u32[]{:S(2)}) copy-start(bf16[256,5,1280]{0,2,1:T(8,128)(2,1)S(1)} %multiply_convert_fusion.1) | copy-start | bytes 9830404
  84.3 2.4 copy-start.14
  85.5 1.9 copy-start.11
  90.5 1.7 copy-start.15
  92.2 1.1 copy-start.1
  92.2 1.5 copy-start.3
  93.7 1.6 copy-start.18
  100.1 5.5 %copy-start.12 = (bf16[256,5,1280]{0,2,1:T(8,128)(2,1)S(1)}, bf16[256,5,1280]{0,2,1:T(8,128)(2,1)}, u32[]{:S(2)}) copy-start(bf16[256,5,1280]{0,2,1:T(8,128)(2,1)} %multiply_convert_fusion.2) | copy-start | bytes 9830404
  102.8 3.4 %copy-start.16 = (bf16[256,5,1280]{0,2,1:T(8,128)(2,1)S(1)}, bf16[256,5,1280]{0,2,1:T(8,128)(2,1)}, u32[]{:S(2)}) copy-start(bf16[256,5,1280]{0,2,1:T(8,128)(2,1)} %copy-done.15) | copy-start | bytes 9830404
  106.9 3.8 %copy-start.2 = (bf16[1280,1,512]{0,2,1:T(8,128)(2,1)S(1)}, bf16[1280,1,512]{0,2,1:T(8,128)(2,1)}, u32[]{:S(2)}) copy-start(bf16[1280,1,512]{0,2,1:T(8,128)(2,1)} %copy-done.1) | copy-start | bytes 3932164
  106.9 3.8 %copy-start.4 = (bf16[1280,1,512]{0,2,1:T(8,128)(2,1)S(1)}, bf16[1280,1,512]{0,2,1:T(8,128)(2,1)}, u32[]{:S(2)}) copy-start(bf16[1280,1,512]{0,2,1:T(8,128)(2,1)} %copy-done.3) | copy-start | bytes 3932164
  108.1 5.4 %copy-start.6 = (f32[1280,128]{0,1:T(8,128)S(1)}, f32[1280,128]{0,1:T(8,128)}, u32[]{:S(2)}) copy-start(f32[1280,128]{0,1:T(8,128)} %copy-done.5) | copy-start | bytes 1966084
Sparse Core Ops, SparseCore 0:
  10.4 44.7 all-gather.1
  95.5 88.0 all-reduce.1
where the time goes:
time: 270 us; the launch traced here: 269 us
  waiting for transfers between devices  107 us (40%)
  blocking collectives  75.6 us (28%)
  matrix products  36.8 us (14%)
  other arithmetic  18.9 us (7%)
  between operations  15.9 us (6%)
  local copies, waits for them, and re-layouts  14.6 us (5%)
    psum x1, blocking collectives, shards(): bias_total = lax.psum(local_term, ('resp', 'prompt'))  75.6 us
    psum x1, waiting for transfers between devices, shards(): lax.psum(prompt_part.astype(jnp.bfloat16), 'resp').astype(jnp.float32)  68.2 us
    all_gather x1, waiting for transfers between devices, shards(): prompt_side = lax.all_gather(own_side, 'resp', axis=0, tiled=True)  38.5 us
    unnamed x54, local copies, waits for them, and re-layouts  14.6 us
    dot_general x4, matrix products, member_pass(): jnp.einsum('rhd,kd->rhk', upstream, value_block, preferred_element_type=j...  8.58 us
    dot_general x4, matrix products, member_pass(): jnp.einsum('rhk,kd->rhd', d_scores, key_block, preferred_element_type=jnp...  6.73 us
    dot_general x4, matrix products, member_pass(): jnp.einsum('rhk,kd->rhd', weights_low, value_block, preferred_element_typ...  6.04 us
    dot_general x4, matrix products, member_pass(): jnp.einsum('rhd,kd->rhk', query_group, key_block, preferred_element_type=...  5.63 us
  transfers between devices with their start and end apart: 2, of which 2 were waited for; matrix products, arithmetic and copies ran while one was open for 9% of the time, Pallas kernels for 0%

commit v1 on v0

v1 whole, which is shorter than its diff:
```python
import functools
import math

import jax
import jax.numpy as jnp
from jax import lax
from jax.experimental import pallas as pl
from jax.experimental.pallas import tpu as pltpu
from jax.sharding import PartitionSpec as P

KVH = 4
HD = 128
GROUP = 5
NEG = -1e30
NT = (((1,), (1,)), ((), ()))
SCALE = HD ** -0.5
LOG2E = math.log2(math.e)
CALLS = ((0, 2), (2, 2))


def dot(a, b):
    return jnp.dot(a, b, preferred_element_type=jnp.float32)


def attend_body(slots, rows, shard, chained, meta, q_ref, do_ref, kvr_ref, kvp_ref, *refs):
    refs = refs[2:] if chained else refs
    ao_ref, dq_ref, dkvr_ref, dkvp_ref = refs[:4]
    k_scr, v_scr, kt_scr, vt_scr, s_scr, p_scr, ds_scr, q_scr, dol_scr = refs[4:]
    prompt = slots * shard
    plen, rlen = meta[0], meta[1]
    kvr = kvr_ref[0]
    k0 = kvr[0:1, :HD].astype(jnp.float32)
    piece = lax.broadcasted_iota(jnp.int32, (shard, HD), 0)
    ones_rows = lax.broadcasted_iota(jnp.int32, (16, shard), 0)
    ones_cols = lax.broadcasted_iota(jnp.int32, (16, shard), 1)
    seen = []
    for s in range(slots):
        kv = kvp_ref[s, 0]
        base = s * shard
        vis = piece + base < plen
        seen.append(vis)
        k = kv[:, :HD].astype(jnp.float32)
        v = jnp.where(vis, kv[:, HD:].astype(jnp.float32), 0.0)
        at = slice(s * shard, (s + 1) * shard)
        k_scr[at, :] = jnp.where(vis, k, k0).astype(jnp.bfloat16)
        v_scr[at, :] = v.astype(jnp.bfloat16)
        kt_scr[:, at] = jnp.where(vis, k, 0.0).T.astype(jnp.bfloat16)
        vt_scr[:HD, at] = v.T.astype(jnp.bfloat16)
        vt_scr[HD:, at] = jnp.where(
            (ones_rows == 0) & (ones_cols + base < plen), 1.0, 0.0
        ).astype(jnp.bfloat16)
    k_scr[prompt:, :] = kvr[:, :HD]
    v_scr[prompt:, :] = kvr[:, HD:]
    kt_scr[:, prompt:] = kvr[:, :HD].astype(jnp.float32).T.astype(jnp.bfloat16)
    vt_scr[:HD, prompt:] = kvr[:, HD:].astype(jnp.float32).T.astype(jnp.bfloat16)
    vt_scr[HD:, prompt:] = jnp.where(
        lax.broadcasted_iota(jnp.int32, (16, rows), 0) == 0, 1.0, 0.0
    ).astype(jnp.bfloat16)
    live = lax.broadcasted_iota(jnp.int32, (1, rows), 1) < rlen
    maxes = {}

    def scores(h):
        q = q_ref[:, h * HD : (h + 1) * HD]
        q_scr[h * rows : (h + 1) * rows, :] = q
        s = lax.dot_general(k_scr[...], q, NT, preferred_element_type=jnp.float32)
        sp = s[:prompt]
        causal = lax.broadcasted_iota(jnp.int32, (rows, rows), 0) <= lax.broadcasted_iota(
            jnp.int32, (rows, rows), 1
        )
        sr = jnp.where(causal, s[prompt:], NEG)
        s_scr[h % 2, :prompt, :] = sp
        s_scr[h % 2, prompt:, :] = sr
        maxes[h] = jnp.maximum(
            jnp.max(sp, axis=0, keepdims=True), jnp.max(sr, axis=0, keepdims=True)
        )

    def exponentials(h):
        e = jnp.exp2((s_scr[h % 2] - maxes[h]) * (SCALE * LOG2E))
        p_scr[:, h * rows : (h + 1) * rows] = e.astype(jnp.bfloat16)

    def outputs(h):
        at = slice(h * rows, (h + 1) * rows)
        lanes = slice(h * HD, (h + 1) * HD)
        p = p_scr[:, at]
        ot = dot(vt_scr[...], p)
        share = jnp.where(live, 1.0 / ot[HD : HD + 1], 0.0)
        normal = ot[:HD] * share
        ao_ref[:, lanes] = normal.T.astype(jnp.bfloat16)
        dol = do_ref[:, lanes].astype(jnp.float32).T * share
        row_dot = jnp.sum(dol * normal, axis=0, keepdims=True)
        dol_scr[at, :] = dol.T.astype(jnp.bfloat16)
        dp = dot(v_scr[...], dol.astype(jnp.bfloat16))
        ds_scr[:, at] = p * (dp - row_dot).astype(jnp.bfloat16)

    def query_grads(h):
        at = slice(h * rows, (h + 1) * rows)
        dqt = dot(kt_scr[...], ds_scr[:, at]) * SCALE
        dq_ref[:, h * HD : (h + 1) * HD] = dqt.T.astype(jnp.bfloat16)

    stages = (scores, exponentials, outputs, query_grads)
    for t in range(GROUP + len(stages) - 1):
        for lag, stage in enumerate(stages):
            if 0 <= t - lag < GROUP:
                stage(t - lag)
    dk = dot(ds_scr[...], q_scr[...]) * SCALE
    dv = dot(p_scr[...], dol_scr[...])
    for s in range(slots):
        at = slice(s * shard, (s + 1) * shard)
        dkvp_ref[s, 0, :, :HD] = jnp.where(seen[s], dk[at], 0.0).astype(jnp.bfloat16)
        dkvp_ref[s, 0, :, HD:] = jnp.where(seen[s], dv[at], 0.0).astype(jnp.bfloat16)
    dkvr_ref[0, :, :HD] = dk[prompt:].astype(jnp.bfloat16)
    dkvr_ref[0, :, HD:] = dv[prompt:].astype(jnp.bfloat16)


def attend(meta, q, do, kvr, kvp, first, count, earlier):
    rows, width = q.shape
    slots, _, shard, _ = kvp.shape
    cols = slots * shard + rows
    wide = GROUP * HD
    bf = jnp.bfloat16
    whole = pl.BlockSpec(memory_space=pl.ANY)
    head = pl.BlockSpec((rows, wide), lambda g, m: (0, first + g))
    grid_spec = pltpu.PrefetchScalarGridSpec(
        num_scalar_prefetch=1,
        grid=(count,),
        in_specs=[
            head,
            head,
            pl.BlockSpec((1, rows, 2 * HD), lambda g, m: (first + g, 0, 0)),
            pl.BlockSpec((slots, 1, shard, 2 * HD), lambda g, m: (0, g, 0, 0)),
        ]
        + [whole] * len(earlier),
        out_specs=[
            head,
            head,
            pl.BlockSpec((1, rows, 2 * HD), lambda g, m: (g, 0, 0)),
            pl.BlockSpec((slots, 1, shard, 2 * HD), lambda g, m: (0, g, 0, 0)),
        ],
        scratch_shapes=[
            pltpu.VMEM((cols, HD), bf),
            pltpu.VMEM((cols, HD), bf),
            pltpu.VMEM((HD, cols), bf),
            pltpu.VMEM((HD + 16, cols), bf),
            pltpu.VMEM((2, cols, rows), jnp.float32),
            pltpu.VMEM((cols, GROUP * rows), bf),
            pltpu.VMEM((cols, GROUP * rows), bf),
            pltpu.VMEM((GROUP * rows, HD), bf),
            pltpu.VMEM((GROUP * rows, HD), bf),
        ],
    )
    return pl.pallas_call(
        functools.partial(attend_body, slots, rows, shard, bool(earlier)),
        grid_spec=grid_spec,
        out_shape=[
            jax.ShapeDtypeStruct((rows, width), bf),
            jax.ShapeDtypeStruct((rows, width), bf),
            jax.ShapeDtypeStruct((count, rows, 2 * HD), bf),
            jax.ShapeDtypeStruct((slots, count, shard, 2 * HD), bf),
        ],
        input_output_aliases={5: 0, 6: 1} if earlier else {},
        compiler_params=pltpu.CompilerParams(vmem_limit_bytes=48 * 2**20),
        cost_estimate=pl.CostEstimate(
            flops=count * 12 * GROUP * rows * cols * HD,
            bytes_accessed=count * 4 * rows * wide * 2,
            transcendentals=count * GROUP * rows * cols,
        ),
        name="attend",
    )(meta, q, do, kvr, kvp, *earlier)


def by_head(pairs, bias):
    rows = pairs.shape[0]
    biased = pairs.astype(jnp.float32) + jnp.stack([jnp.zeros_like(bias), bias])
    split = biased.astype(jnp.bfloat16).reshape(rows, 2, KVH, HD)
    return split.transpose(2, 0, 1, 3).reshape(KVH, rows, 2 * HD)


def by_pair(heads):
    rows = heads.shape[1]
    return heads.reshape(KVH, rows, 2, HD).transpose(1, 2, 0, 3).reshape(rows, 2, KVH * HD)


def sum_over(term, axis, size):
    step = 1
    while step < size:
        term = term + lax.ppermute(term, axis, [(i, i ^ step) for i in range(size)])
        step *= 2
    return term


def shards(resp_q, resp_kv, prompt_kv, bias, prompt_len, resp_len, d_out):
    members, prompts = lax.axis_size("resp"), lax.axis_size("prompt")
    own = by_head(prompt_kv[0], bias)
    shard = own.shape[1]
    resp_side = by_head(resp_kv[0, 0], bias)
    gathered = [
        lax.all_to_all(
            jnp.broadcast_to(own[None, first : first + count], (members, count, shard, 2 * HD)), "resp", 0, 0
        )
        for first, count in CALLS
    ]
    queries, cotangent = resp_q[0, 0], d_out[0, 0]
    rows = queries.shape[0]
    meta = jnp.concatenate([prompt_len, resp_len[0]]).astype(jnp.int32)
    live = jnp.arange(rows, dtype=jnp.int32) < resp_len[0, 0]
    live_sum = jnp.sum(jnp.where(live[:, None], cotangent.astype(jnp.float32), 0.0), axis=0)
    term = jnp.sum(live_sum.reshape(KVH, GROUP, HD), axis=1).reshape(KVH * HD)
    term = sum_over(sum_over(term, "prompt", prompts), "resp", members)
    d_bias = term / (members * prompts)
    earlier, resp_grads, prompt_grads = (), [], []
    for (first, count), kvp in zip(CALLS, gathered):
        *earlier, resp_grad, part = attend(
            meta, queries, cotangent, resp_side, kvp, first, count, tuple(earlier)
        )
        resp_grads.append(resp_grad)
        arrived = lax.all_to_all(part, "resp", 0, 0)
        prompt_grads.append(jnp.sum(arrived.astype(jnp.float32), axis=0).astype(jnp.bfloat16))
    attn_out, d_q = earlier
    return (
        attn_out[None, None],
        d_q[None, None],
        by_pair(jnp.concatenate(resp_grads))[None, None],
        by_pair(jnp.concatenate(prompt_grads))[None],
        d_bias,
    )


def solution(mesh):
    return jax.shard_map(
        shards,
        mesh=mesh,
        in_specs=(
            P("prompt", "resp", None, None),
            P("prompt", "resp", None, None, None),
            P("prompt", "resp", None, None),
            P(),
            P("prompt"),
            P("prompt", "resp"),
            P("prompt", "resp", None, None),
        ),
        out_specs=(
            P("prompt", "resp", None, None),
            P("prompt", "resp", None, None),
            P("prompt", "resp", None, None, None),
            P("prompt", "resp", None, None),
            P(),
        ),
        check_vma=False,
    )
```

time: 270 us -> 133 us (0.49)
  waiting for transfers between devices: 107 us -> 31.1 us
  blocking collectives: 75.6 us -> 19.7 us
  matrix products: 36.8 us -> 0 us
  starting transfers between devices: 0.08 us -> 34.1 us
  Pallas kernels: 0 us -> 28 us
  other arithmetic: 18.9 us -> 2.9 us
  between operations: 15.9 us -> 2.1 us
    psum x1 -> x0, blocking collectives: 75.6 us -> none  [shards(): bias_total = lax.psum(local_term, ('resp', 'prompt'))]
    psum x1 -> x0, waiting for transfers between devices: 68.2 us -> none  [shards(): lax.psum(prompt_part.astype(jnp.bfloat16), 'resp').astype(jnp.float32)]
    all_gather x1 -> x0, waiting for transfers between devices: 38.5 us -> none  [shards(): prompt_side = lax.all_gather(own_side, 'resp', axis=0, tiled=True)]
    dot_general x24 -> x0, matrix products: 36.8 us -> none  [the longest x4 8.58 us: member_pass(): jnp.einsum('rhd,kd->rhk', upstream, value_block, preferred_element_type=j...]
    pallas_call x0 -> x2, Pallas kernels: none -> 28 us  [attend(): pl.pallas_call(functools.partial(attend_body, slots, rows, shard, bool(ea...]
    all_to_all x0 -> x1, blocking collectives: none -> 19.7 us  [shards(): arrived = lax.all_to_all(part, 'resp', 0, 0)]
    ppermute x0 -> x8, starting transfers between devices: none -> 18.7 us  [sum_over(): term = term + lax.ppermute(term, axis, [(i, i ^ step) for i in range(size)])]
    ppermute x0 -> x8, waiting for transfers between devices: none -> 16.7 us  [sum_over(): term = term + lax.ppermute(term, axis, [(i, i ^ step) for i in range(size)])]
  transfers between devices with their start and end apart: 2 -> 11, of which waited for: 2 -> 9; matrix products, arithmetic and copies ran while one was open for 9% -> 6% of each run, Pallas kernels for 0% -> 11%
where the time goes in v1:
time: 133 us
  starting transfers between devices  34.1 us (26%)
  waiting for transfers between devices  31.1 us (23%)
  Pallas kernels  28 us (21%)
  blocking collectives  19.7 us (15%)
  local copies, waits for them, and re-layouts  15 us (11%)
  other arithmetic  2.9 us (2%)
  between operations  2.1 us (2%)
    pallas_call x2, Pallas kernels, attend(): pl.pallas_call(functools.partial(attend_body, slots, rows, shard, bool(ea...  28 us
    all_to_all x1, blocking collectives, shards(): arrived = lax.all_to_all(part, 'resp', 0, 0)  19.7 us
    ppermute x8, starting transfers between devices, sum_over(): term = term + lax.ppermute(term, axis, [(i, i ^ step) for i in range(size)])  18.7 us
    ppermute x8, waiting for transfers between devices, sum_over(): term = term + lax.ppermute(term, axis, [(i, i ^ step) for i in range(size)])  16.7 us
    all_to_all x2, waiting for transfers between devices, shards(): lax.all_to_all(jnp.broadcast_to(own[None, first:first + count], (members,...  14.4 us
    all_to_all x2, starting transfers between devices, shards(): lax.all_to_all(jnp.broadcast_to(own[None, first:first + count], (members,...  10.6 us
    unnamed x20, local copies, waits for them, and re-layouts  6.14 us
    all_to_all x1, starting transfers between devices, shards(): arrived = lax.all_to_all(part, 'resp', 0, 0)  4.76 us
  transfers between devices with their start and end apart: 11, of which 9 were waited for; matrix products, arithmetic and copies ran while one was open for 6% of the time, Pallas kernels for 11%

profile of v1, /device:TPU:2, one launch (start us, length us, event | category | flops | bytes accessed | tf_op | source)
XLA Modules:
  0.0 132.8 jit_solution(3431148791711601989)
XLA Ops:
  1.3 1.2 reshape.54
  3.0 1.1 broadcast_in_dim.40
  4.1 5.8 %all-to-all-start.1 = ((bf16[8,2,128,256]{3,2,1,0:T(8,128)(2,1)}), bf16[8,2,128,256]{3,2,1,0:T(8,128)(2,1)S(1)}, u32[]{:S(2)}, u32[]{:S(2)}) async-start(bf16[8,2,128,256]{3,2,1,0:T(8,128)(2,1)} %broadcast_in_dim.40), calls=%async_computation.1 | async-start | bytes 2097152 | tf_op jit(solution)/shard_map/all_to_all | solution.py:197
  10.1 14.4 %all-to-all-done.1.kvp_ref = bf16[8,2,128,256]{3,2,1,0:T(8,128)(2,1)S(1)} async-done(((bf16[8,2,128,256]{3,2,1,0:T(8,128)(2,1)}), bf16[8,2,128,256]{3,2,1,0:T(8,128)(2,1)S(1)}, u32[]{:S(2)}, u32[]{:S(2)}) %all-to-all-start.1) | async-done | bytes 1048608 | tf_op jit(solution)/shard_map/all_to_all | solution.py:197
  24.4 1.1 broadcast_in_dim.38
  25.5 4.8 %all-to-all-start = ((bf16[8,2,128,256]{3,2,1,0:T(8,128)(2,1)}), bf16[8,2,128,256]{3,2,1,0:T(8,128)(2,1)S(1)}, u32[]{:S(2)}, u32[]{:S(2)}) async-start(bf16[8,2,128,256]{3,2,1,0:T(8,128)(2,1)} %broadcast_in_dim.38), calls=%async_computation | async-start | bytes 2097152 | tf_op jit(solution)/shard_map/all_to_all | solution.py:197
  31.6 1.2 copy.46
  32.9 2.3 %copy.47 = f32[256,2,4,128]{3,0,2,1:T(8,128)} copy(bf16[256,2,4,128]{0,3,2,1:T(8,128)(2,1)} %bitcast.31) | data formatting | bytes 1572864 | tf_op jit(solution)/shard_map/convert_element_type | solution.py:173
  35.3 1.4 %copy_bitcast_fusion.kvr_ref = bf16[4,256,256]{2,1,0:T(8,128)(2,1)S(1)} fusion(f32[256,2,4,128]{3,0,2,1:T(8,128)} %copy.47, f32[2,4,128]{2,1,0:T(4,128)S(1)} %add.46), kind=kLoop, calls=%fused_computation.3 | loop fusion | flops 524288 | bytes 1576960 | tf_op jit(solution)/shard_map/reshape | solution.py:175
  36.8 14.0 %attend.2 = (bf16[256,2560]{1,0:T(8,128)(2,1)}, bf16[256,2560]{1,0:T(8,128)(2,1)}, bf16[2,256,256]{2,1,0:T(8,128)(2,1)S(1)}, bf16[8,2,128,256]{3,2,1,0:T(8,128)(2,1)}) custom-call(s32[2]{0:T(128)S(1)} %pad_add_fusion.meta, bf16[256,2560]{1,0:T(8,128)(2,1)S(1)} %bitcast.29, bf16[256,2560]{1,0:T(8,128)(2,1)S(1)} %bitcast.27, ...), custom_call_target="tpu_custom_call" | custom-call | flops 5033164800 | bytes 2621440 | tf_op jit(solution)/shard_map/attend/pallas_call | solution.py:151
  50.8 0.8 copy-done.1
  52.3 1.0 copy-done.2
  53.3 1.3 copy-done.6
  54.7 14.0 %attend.3 = (bf16[256,2560]{1,0:T(8,128)(2,1)}, bf16[256,2560]{1,0:T(8,128)(2,1)}, bf16[2,256,256]{2,1,0:T(8,128)(2,1)S(1)}, bf16[8,2,128,256]{3,2,1,0:T(8,128)(2,1)S(1)}) custom-call(s32[2]{0:T(128)S(1)} %pad_add_fusion.meta, bf16[256,2560]{1,0:T(8,128)(2,1)S(1)} %bitcast.30, ...), custom_call_target="tpu_custom_call", output_to_operand_aliasing={{0}: (5, {}), {1}: (6, {})} | custom-call | flops 5033164800 | bytes 2621440 | tf_op jit(solution)/shard_map/attend/pallas_call | solution.py:151
  68.6 19.7 %all_to_all.20 = bf16[8,2,128,256]{3,2,1,0:T(8,128)(2,1)} all-to-all(bf16[8,2,128,256]{3,2,1,0:T(8,128)(2,1)S(1)} %get-tuple-element.20), channel_id=1, replica_groups=mesh['resp'=8,'prompt'=32] {'resp'}, dimensions={0} | all-to-all | bytes 2097152 | tf_op jit(solution)/shard_map/all_to_all | solution.py:216
  88.4 4.8 %all-to-all-start.2 = ((bf16[8,2,128,256]{3,2,1,0:T(8,128)(2,1)}), bf16[8,2,128,256]{3,2,1,0:T(8,128)(2,1)S(1)}, u32[]{:S(2)}, u32[]{:S(2)}) async-start(bf16[8,2,128,256]{3,2,1,0:T(8,128)(2,1)} %get-tuple-element.19), calls=%async_computation.2 | async-start | bytes 2097152 | tf_op jit(solution)/shard_map/all_to_all | solution.py:216
  93.6 1.1 collective-permute-done
  94.8 1.9 %collective-permute-start.1 = (f32[512]{0:T(512)S(1)}, f32[512]{0:T(512)S(1)}, u32[]{:S(2)}, u32[]{:S(2)}) collective-permute-start(f32[512]{0:T(512)S(1)} %bitcast_add_fusion), channel_id=1, source_target_pairs={{0,2},{1,3},{2,0},{3,1},{4,6},{5,7},{6,4},{7,5},{8,10},{9,11},{10,... | collective-permute-start | bytes 6152 | tf_op jit(solution)/shard_map/ppermute | solution.py:186
  96.7 1.7 %collective-permute-done.1 = f32[512]{0:T(512)S(1)} collective-permute-done((f32[512]{0:T(512)S(1)}, f32[512]{0:T(512)S(1)}, u32[]{:S(2)}, u32[]{:S(2)}) %collective-permute-start.1) | collective-permute-done | bytes 2080 | tf_op jit(solution)/shard_map/ppermute | solution.py:186
  98.3 3.3 %collective-permute-start.2 = (f32[512]{0:T(512)S(1)}, f32[512]{0:T(512)S(1)}, u32[]{:S(2)}, u32[]{:S(2)}) collective-permute-start(f32[512]{0:T(512)S(1)} %add.52), channel_id=1, source_target_pairs={{0,4},{1,5},{2,6},{3,7},{4,0},{5,1},{6,2},{7,3},{8,12},{9,13},{10,... | collective-permute-start | bytes 6152 | tf_op jit(solution)/shard_map/ppermute | solution.py:186
  101.6 1.6 %collective-permute-done.2 = f32[512]{0:T(512)S(1)} collective-permute-done((f32[512]{0:T(512)S(1)}, f32[512]{0:T(512)S(1)}, u32[]{:S(2)}, u32[]{:S(2)}) %collective-permute-start.2) | collective-permute-done | bytes 2080 | tf_op jit(solution)/shard_map/ppermute | solution.py:186
  103.2 6.8 %collective-permute-start.3 = (f32[512]{0:T(512)S(1)}, f32[512]{0:T(512)S(1)}, u32[]{:S(2)}, u32[]{:S(2)}) collective-permute-start(f32[512]{0:T(512)S(1)} %add.53), channel_id=1, source_target_pairs={{0,8},{1,9},{2,10},{3,11},{4,12},{5,13},{6,14},{7,15},{8,0},{9,1},... | collective-permute-start | bytes 6152 | tf_op jit(solution)/shard_map/ppermute | solution.py:186
  110.0 1.6 %collective-permute-done.3 = f32[512]{0:T(512)S(1)} collective-permute-done((f32[512]{0:T(512)S(1)}, f32[512]{0:T(512)S(1)}, u32[]{:S(2)}, u32[]{:S(2)}) %collective-permute-start.3) | collective-permute-done | bytes 2080 | tf_op jit(solution)/shard_map/ppermute | solution.py:186
  111.6 2.9 %collective-permute-start.4 = (f32[512]{0:T(512)S(1)}, f32[512]{0:T(512)S(1)}, u32[]{:S(2)}, u32[]{:S(2)}) collective-permute-start(f32[512]{0:T(512)S(1)} %add.54), channel_id=1, source_target_pairs={{0,16},{1,17},{2,18},{3,19},{4,20},{5,21},{6,22},{7,23},{8,24},{9,... | collective-permute-start | bytes 6152 | tf_op jit(solution)/shard_map/ppermute | solution.py:186
  114.5 2.2 %collective-permute-done.4 = f32[512]{0:T(512)S(1)} collective-permute-done((f32[512]{0:T(512)S(1)}, f32[512]{0:T(512)S(1)}, u32[]{:S(2)}, u32[]{:S(2)}) %collective-permute-start.4) | collective-permute-done | bytes 2080 | tf_op jit(solution)/shard_map/ppermute | solution.py:186
  116.8 3.5 %collective-permute-done.5 = f32[512]{0:T(512)S(1)} collective-permute-done((f32[512]{0:T(512)S(1)}, f32[512]{0:T(512)S(1)}, u32[]{:S(2)}, u32[]{:S(2)}) %collective-permute-start.5) | collective-permute-done | bytes 2080 | tf_op jit(solution)/shard_map/ppermute | solution.py:186
  120.3 2.1 %collective-permute-start.6 = (f32[512]{0:T(512)S(1)}, f32[512]{0:T(512)S(1)}, u32[]{:S(2)}, u32[]{:S(2)}) collective-permute-start(f32[512]{0:T(512)S(1)} %add.56), channel_id=1, source_target_pairs={{0,64},{32,96},{64,0},{96,32},{128,192},{160,224},{192,128},{224,1... | collective-permute-start | bytes 6152 | tf_op jit(solution)/shard_map/ppermute | solution.py:186
  122.4 3.0 %collective-permute-done.6 = f32[512]{0:T(512)S(1)} collective-permute-done((f32[512]{0:T(512)S(1)}, f32[512]{0:T(512)S(1)}, u32[]{:S(2)}, u32[]{:S(2)}) %collective-permute-start.6) | collective-permute-done | bytes 2080 | tf_op jit(solution)/shard_map/ppermute | solution.py:186
  125.4 1.5 %collective-permute-start.7 = (f32[512]{0:T(512)S(1)}, f32[512]{0:T(512)S(1)}, u32[]{:S(2)}, u32[]{:S(2)}) collective-permute-start(f32[512]{0:T(512)S(1)} %add.57), channel_id=1, source_target_pairs={{0,128},{32,160},{64,192},{96,224},{128,0},{160,32},{192,64},{224,... | collective-permute-start | bytes 6152 | tf_op jit(solution)/shard_map/ppermute | solution.py:186
  126.9 2.1 %collective-permute-done.7 = f32[512]{0:T(512)S(1)} collective-permute-done((f32[512]{0:T(512)S(1)}, f32[512]{0:T(512)S(1)}, u32[]{:S(2)}, u32[]{:S(2)}) %collective-permute-start.7) | collective-permute-done | bytes 2080 | tf_op jit(solution)/shard_map/ppermute | solution.py:186
  130.4 1.0 broadcast_in_dim_reshape.6
  132.0 0.9 copy.54
  (48 shorter events, 4.8 us)
Async XLA Ops:
  4.1 20.4 %all-to-all-start.1 = ((bf16[8,2,128,256]{3,2,1,0:T(8,128)(2,1)}), bf16[8,2,128,256]{3,2,1,0:T(8,128)(2,1)S(1)}, u32[]{:S(2)}, u32[]{:S(2)}) async-start(bf16[8,2,128,256]{3,2,1,0:T(8,128)(2,1)} %broadcast_in_dim.40), calls=%async_computation.1 | async-start | bytes 2097152 | tf_op jit(solution)/shard_map/all_to_all | solution.py:197
  25.5 6.1 %copy-start.8 = (bf16[1,1,256,2,512]{4,3,2,1,0:T(2,128)(2,1)S(1)}, bf16[1,1,256,2,512]{4,3,2,1,0:T(2,128)(2,1)}, u32[]{:S(2)}) copy-start(bf16[1,1,256,2,512]{4,3,2,1,0:T(2,128)(2,1)} %param.8) | copy-start | bytes 1572868
  25.5 26.7 %all-to-all-start = ((bf16[8,2,128,256]{3,2,1,0:T(8,128)(2,1)}), bf16[8,2,128,256]{3,2,1,0:T(8,128)(2,1)S(1)}, u32[]{:S(2)}, u32[]{:S(2)}) async-start(bf16[8,2,128,256]{3,2,1,0:T(8,128)(2,1)} %broadcast_in_dim.38), calls=%async_computation | async-start | bytes 2097152 | tf_op jit(solution)/shard_map/all_to_all | solution.py:197
  32.9 3.8 %copy-start = (bf16[1,1,256,2560]{3,2,1,0:T(8,128)(2,1)S(1)}, bf16[1,1,256,2560]{3,2,1,0:T(8,128)(2,1)}, u32[]{:S(2)}) copy-start(bf16[1,1,256,2560]{3,2,1,0:T(8,128)(2,1)} %param.13) | copy-start | bytes 3932164
  35.2 1.6 %copy-start.5 = (bf16[1,1,256,2560]{3,2,1,0:T(8,128)(2,1)S(1)}, bf16[1,1,256,2560]{3,2,1,0:T(8,128)(2,1)}, u32[]{:S(2)}) copy-start(bf16[1,1,256,2560]{3,2,1,0:T(8,128)(2,1)} %param.7) | copy-start | bytes 3932164
  50.8 0.8 copy-start.1
  51.6 0.7 copy-start.3
  52.3 1.0 copy-start.2
  53.3 1.3 copy-start.6
  88.4 41.2 %copy-start.4 = (bf16[2,256,256]{2,1,0:T(8,128)(2,1)S(1)}, bf16[2,256,256]{2,1,0:T(8,128)(2,1)}, u32[]{:S(2)}) copy-start(bf16[2,256,256]{2,1,0:T(8,128)(2,1)} %copy-done.3) | copy-start | bytes 786436
  88.4 43.2 %all-to-all-start.2 = ((bf16[8,2,128,256]{3,2,1,0:T(8,128)(2,1)}), bf16[8,2,128,256]{3,2,1,0:T(8,128)(2,1)S(1)}, u32[]{:S(2)}, u32[]{:S(2)}) async-start(bf16[8,2,128,256]{3,2,1,0:T(8,128)(2,1)} %get-tuple-element.19), calls=%async_computation.2 | async-start | bytes 2097152 | tf_op jit(solution)/shard_map/all_to_all | solution.py:216
  93.5 1.2 collective-permute-start
  94.8 3.6 %collective-permute-start.1 = (f32[512]{0:T(512)S(1)}, f32[512]{0:T(512)S(1)}, u32[]{:S(2)}, u32[]{:S(2)}) collective-permute-start(f32[512]{0:T(512)S(1)} %bitcast_add_fusion), channel_id=1, source_target_pairs={{0,2},{1,3},{2,0},{3,1},{4,6},{5,7},{6,4},{7,5},{8,10},{9,11},{10,... | collective-permute-start | bytes 6152 | tf_op jit(solution)/shard_map/ppermute | solution.py:186
  98.3 4.8 %collective-permute-start.2 = (f32[512]{0:T(512)S(1)}, f32[512]{0:T(512)S(1)}, u32[]{:S(2)}, u32[]{:S(2)}) collective-permute-start(f32[512]{0:T(512)S(1)} %add.52), channel_id=1, source_target_pairs={{0,4},{1,5},{2,6},{3,7},{4,0},{5,1},{6,2},{7,3},{8,12},{9,13},{10,... | collective-permute-start | bytes 6152 | tf_op jit(solution)/shard_map/ppermute | solution.py:186
  103.2 8.4 %collective-permute-start.3 = (f32[512]{0:T(512)S(1)}, f32[512]{0:T(512)S(1)}, u32[]{:S(2)}, u32[]{:S(2)}) collective-permute-start(f32[512]{0:T(512)S(1)} %add.53), channel_id=1, source_target_pairs={{0,8},{1,9},{2,10},{3,11},{4,12},{5,13},{6,14},{7,15},{8,0},{9,1},... | collective-permute-start | bytes 6152 | tf_op jit(solution)/shard_map/ppermute | solution.py:186
  111.6 5.1 %collective-permute-start.4 = (f32[512]{0:T(512)S(1)}, f32[512]{0:T(512)S(1)}, u32[]{:S(2)}, u32[]{:S(2)}) collective-permute-start(f32[512]{0:T(512)S(1)} %add.54), channel_id=1, source_target_pairs={{0,16},{1,17},{2,18},{3,19},{4,20},{5,21},{6,22},{7,23},{8,24},{9,... | collective-permute-start | bytes 6152 | tf_op jit(solution)/shard_map/ppermute | solution.py:186
  116.7 3.6 %collective-permute-start.5 = (f32[512]{0:T(512)S(1)}, f32[512]{0:T(512)S(1)}, u32[]{:S(2)}, u32[]{:S(2)}) collective-permute-start(f32[512]{0:T(512)S(1)} %add.55), channel_id=1, source_target_pairs={{0,32},{32,0},{64,96},{96,64},{128,160},{160,128},{192,224},{224,1... | collective-permute-start | bytes 6152 | tf_op jit(solution)/shard_map/ppermute | solution.py:186
  120.3 5.1 %collective-permute-start.6 = (f32[512]{0:T(512)S(1)}, f32[512]{0:T(512)S(1)}, u32[]{:S(2)}, u32[]{:S(2)}) collective-permute-start(f32[512]{0:T(512)S(1)} %add.56), channel_id=1, source_target_pairs={{0,64},{32,96},{64,0},{96,32},{128,192},{160,224},{192,128},{224,1... | collective-permute-start | bytes 6152 | tf_op jit(solution)/shard_map/ppermute | solution.py:186
  125.4 3.6 %collective-permute-start.7 = (f32[512]{0:T(512)S(1)}, f32[512]{0:T(512)S(1)}, u32[]{:S(2)}, u32[]{:S(2)}) collective-permute-start(f32[512]{0:T(512)S(1)} %add.57), channel_id=1, source_target_pairs={{0,128},{32,160},{64,192},{96,224},{128,0},{160,32},{192,64},{224,... | collective-permute-start | bytes 6152 | tf_op jit(solution)/shard_map/ppermute | solution.py:186
  129.7 1.7 %copy-start.7 = (bf16[8,2,128,256]{3,2,1,0:T(8,128)(2,1)S(1)}, bf16[8,2,128,256]{3,2,1,0:T(8,128)(2,1)}, u32[]{:S(2)}) copy-start(bf16[8,2,128,256]{3,2,1,0:T(8,128)(2,1)} %all_to_all.20) | copy-start | bytes 3145732

commit v2 on v1

--- a/solution.py
+++ b/solution.py
@@ -16,16 +16,22 @@
 SCALE = HD ** -0.5
 LOG2E = math.log2(math.e)
 CALLS = ((0, 2), (2, 2))
+EXTRA = 16
+HEAD_STEPS, TAIL_STEPS = (4, 16), (1, 2, 8)
 
 
 def dot(a, b):
     return jnp.dot(a, b, preferred_element_type=jnp.float32)
 
 
-def attend_body(slots, rows, shard, chained, meta, q_ref, do_ref, kvr_ref, kvp_ref, *refs):
-    refs = refs[2:] if chained else refs
-    ao_ref, dq_ref, dkvr_ref, dkvp_ref = refs[:4]
-    k_scr, v_scr, kt_scr, vt_scr, s_scr, p_scr, ds_scr, q_scr, dol_scr = refs[4:]
+def attend_body(slots, rows, shard, term, chained, meta, q_ref, do_ref, kvr_ref, *refs):
+    pieces, refs = refs[:slots], refs[slots:]
+    if term:
+        term_ref, refs = refs[0], refs[1:]
+    refs = refs[chained:]
+    ao_ref, dq_ref, dkvr_ref, parts_ref = refs[:4]
+    refs = refs[4:]
+    k_scr, v_scr, kt_scr, vt_scr, s_scr, p_scr, ds_scr, q_scr, dol_scr = refs
     prompt = slots * shard
     plen, rlen = meta[0], meta[1]
     kvr = kvr_ref[0]
@@ -35,8 +41,8 @@
     ones_cols = lax.broadcasted_iota(jnp.int32, (16, shard), 1)
     seen = []
     for s in range(slots):
-        kv = kvp_ref[s, 0]
-        base = s * shard
+        kv = pieces[s][0]
+        base = meta[2 + s] * shard
         vis = piece + base < plen
         seen.append(vis)
         k = kv[:, :HD].astype(jnp.float32)
@@ -106,35 +112,41 @@
     dv = dot(p_scr[...], dol_scr[...])
     for s in range(slots):
         at = slice(s * shard, (s + 1) * shard)
-        dkvp_ref[s, 0, :, :HD] = jnp.where(seen[s], dk[at], 0.0).astype(jnp.bfloat16)
-        dkvp_ref[s, 0, :, HD:] = jnp.where(seen[s], dv[at], 0.0).astype(jnp.bfloat16)
+        out = parts_ref.at[meta[2 + s], 0]
+        if term:
+            out[shard:, :] = term_ref[...]
+        out[:shard, :HD] = jnp.where(seen[s], dk[at], 0.0).astype(jnp.bfloat16)
+        out[:shard, HD:] = jnp.where(seen[s], dv[at], 0.0).astype(jnp.bfloat16)
     dkvr_ref[0, :, :HD] = dk[prompt:].astype(jnp.bfloat16)
     dkvr_ref[0, :, HD:] = dv[prompt:].astype(jnp.bfloat16)
 
 
-def attend(meta, q, do, kvr, kvp, first, count, earlier):
+def placed(space, *arrays):
+    return [pltpu.with_memory_space_constraint(a, space) for a in arrays]
+
+
+def attend(meta, q, do, kvr, pieces, first, count, term, earlier):
     rows, width = q.shape
-    slots, _, shard, _ = kvp.shape
+    slots, shard = len(pieces), pieces[0].shape[1]
     cols = slots * shard + rows
     wide = GROUP * HD
     bf = jnp.bfloat16
     whole = pl.BlockSpec(memory_space=pl.ANY)
     head = pl.BlockSpec((rows, wide), lambda g, m: (0, first + g))
+    piece = pl.BlockSpec((1, shard, 2 * HD), lambda g, m: (first + g, 0, 0))
+    part = (slots, count, shard + sum(t.shape[0] for t in term), 2 * HD)
     grid_spec = pltpu.PrefetchScalarGridSpec(
         num_scalar_prefetch=1,
         grid=(count,),
-        in_specs=[
-            head,
-            head,
-            pl.BlockSpec((1, rows, 2 * HD), lambda g, m: (first + g, 0, 0)),
-            pl.BlockSpec((slots, 1, shard, 2 * HD), lambda g, m: (0, g, 0, 0)),
-        ]
+        in_specs=[head, head, pl.BlockSpec((1, rows, 2 * HD), lambda g, m: (first + g, 0, 0))]
+        + [piece] * slots
+        + [pl.BlockSpec(t.shape, lambda g, m: (0, 0)) for t in term]
         + [whole] * len(earlier),
         out_specs=[
             head,
             head,
             pl.BlockSpec((1, rows, 2 * HD), lambda g, m: (g, 0, 0)),
-            pl.BlockSpec((slots, 1, shard, 2 * HD), lambda g, m: (0, g, 0, 0)),
+            pl.BlockSpec((slots, 1, *part[2:]), lambda g, m: (0, g, 0, 0)),
         ],
         scratch_shapes=[
             pltpu.VMEM((cols, HD), bf),
@@ -148,24 +160,51 @@
             pltpu.VMEM((GROUP * rows, HD), bf),
         ],
     )
-    return pl.pallas_call(
-        functools.partial(attend_body, slots, rows, shard, bool(earlier)),
+    aliases = {4 + slots + len(term) + i: i for i in range(len(earlier))}
+    ao, dq, resp_grad, parts = pl.pallas_call(
+        functools.partial(attend_body, slots, rows, shard, len(term), len(earlier)),
         grid_spec=grid_spec,
         out_shape=[
             jax.ShapeDtypeStruct((rows, width), bf),
             jax.ShapeDtypeStruct((rows, width), bf),
             jax.ShapeDtypeStruct((count, rows, 2 * HD), bf),
-            jax.ShapeDtypeStruct((slots, count, shard, 2 * HD), bf),
+            pltpu.HBM(part, bf),
         ],
-        input_output_aliases={5: 0, 6: 1} if earlier else {},
-        compiler_params=pltpu.CompilerParams(vmem_limit_bytes=48 * 2**20),
+        input_output_aliases=aliases,
+        compiler_params=pltpu.CompilerParams(vmem_limit_bytes=28 * 2**20),
         cost_estimate=pl.CostEstimate(
             flops=count * 12 * GROUP * rows * cols * HD,
             bytes_accessed=count * 4 * rows * wide * 2,
             transcendentals=count * GROUP * rows * cols,
         ),
         name="attend",
-    )(meta, q, do, kvr, kvp, *earlier)
+    )(meta, *placed(pltpu.HBM, q, do), *placed(pltpu.HBM if earlier else pltpu.VMEM, kvr, *pieces), *term, *earlier)
+    return (ao, dq), resp_grad, parts
+
+
+def relay_body(parts_ref, held_ref, own_ref, term_ref, held_out):
+    shard = own_ref.shape[1]
+    total = jnp.sum(parts_ref[...].astype(jnp.float32), axis=0)
+    own_ref[...] = total[:, :shard]
+    extras = total[0, shard:]
+    term_ref[...] = extras[0:2] + extras[2:4] + extras[4:6]
+
+
+def relay(parts, held):
+    vmem, whole = pl.BlockSpec(memory_space=pltpu.VMEM), pl.BlockSpec(memory_space=pl.ANY)
+    _, count, padded, width = parts.shape
+    return pl.pallas_call(
+        relay_body,
+        in_specs=[vmem, whole],
+        out_specs=[vmem, vmem, whole],
+        out_shape=[
+            jax.ShapeDtypeStruct((count, padded - EXTRA, width), jnp.float32),
+            jax.ShapeDtypeStruct((2, width), jnp.float32),
+            jax.ShapeDtypeStruct(held.shape, held.dtype),
+        ],
+        input_output_aliases={1: 2},
+        name="relay",
+    )(*placed(pltpu.VMEM, parts), *placed(pltpu.HBM, held))
 
 
 def by_head(pairs, bias):
@@ -180,47 +219,75 @@
     return heads.reshape(KVH, rows, 2, HD).transpose(1, 2, 0, 3).reshape(rows, 2, KVH * HD)
 
 
-def sum_over(term, axis, size):
-    step = 1
-    while step < size:
-        term = term + lax.ppermute(term, axis, [(i, i ^ step) for i in range(size)])
-        step *= 2
-    return term
+def move(value, dy, dx, sizes):
+    ny, nx = sizes
+    return lax.ppermute(
+        value,
+        "resp",
+        [(y * nx + x, (y + dy) % ny * nx + (x + dx) % nx) for y in range(ny) for x in range(nx)],
+    )
+
+
+def gather_pieces(own, sizes):
+    beside = move(own, 1, 0, sizes)
+    left, right = move(own, 0, 1, sizes), move(own, 0, -1, sizes)
+    beside_left, beside_right = move(beside, 0, 1, sizes), move(right, 1, 0, sizes)
+    opposite = move(right, 0, -1, sizes)
+    beside_opposite = move(opposite, 1, 0, sizes)
+    return [own, beside, left, right, beside_left, beside_right, opposite, beside_opposite]
+
+
+PLACES = ((0, 0), (1, 0), (0, -1), (0, 1), (1, -1), (1, 1), (0, 2), (1, 2))
+
+def exchange_sum(term, axis, step):
+    size = lax.axis_size(axis)
+    return term + lax.ppermute(term, axis, [(i, i ^ step) for i in range(size)])
+
+
+def three_parts(value):
+    parts = []
+    for _ in range(3):
+        high = lax.reduce_precision(value, 8, 7)
+        parts.append(high.astype(jnp.bfloat16))
+        value = value - high
+    return jnp.stack(parts)
 
 
 def shards(resp_q, resp_kv, prompt_kv, bias, prompt_len, resp_len, d_out):
     members, prompts = lax.axis_size("resp"), lax.axis_size("prompt")
+    sizes = (2, members // 2)
     own = by_head(prompt_kv[0], bias)
-    shard = own.shape[1]
-    resp_side = by_head(resp_kv[0, 0], bias)
-    gathered = [
-        lax.all_to_all(
-            jnp.broadcast_to(own[None, first : first + count], (members, count, shard, 2 * HD)), "resp", 0, 0
-        )
-        for first, count in CALLS
-    ]
     queries, cotangent = resp_q[0, 0], d_out[0, 0]
     rows = queries.shape[0]
-    meta = jnp.concatenate([prompt_len, resp_len[0]]).astype(jnp.int32)
     live = jnp.arange(rows, dtype=jnp.int32) < resp_len[0, 0]
     live_sum = jnp.sum(jnp.where(live[:, None], cotangent.astype(jnp.float32), 0.0), axis=0)
-    term = jnp.sum(live_sum.reshape(KVH, GROUP, HD), axis=1).reshape(KVH * HD)
-    term = sum_over(sum_over(term, "prompt", prompts), "resp", members)
-    d_bias = term / (members * prompts)
-    earlier, resp_grads, prompt_grads = (), [], []
-    for (first, count), kvp in zip(CALLS, gathered):
-        *earlier, resp_grad, part = attend(
-            meta, queries, cotangent, resp_side, kvp, first, count, tuple(earlier)
-        )
-        resp_grads.append(resp_grad)
-        arrived = lax.all_to_all(part, "resp", 0, 0)
-        prompt_grads.append(jnp.sum(arrived.astype(jnp.float32), axis=0).astype(jnp.bfloat16))
-    attn_out, d_q = earlier
+    term = jnp.sum(live_sum.reshape(KVH, GROUP, HD), axis=1)
+    pieces = gather_pieces(own, sizes)
+    term = exchange_sum(term, "prompt", HEAD_STEPS[0])
+    arrived = pieces[4][0, :1, :HD].astype(jnp.float32) + pieces[5][0, :1, :HD].astype(jnp.float32)
+    term = exchange_sum(term + 0.0 * arrived, "prompt", HEAD_STEPS[1])
+    term = jnp.pad(three_parts(term).reshape(6, 2 * HD), ((0, EXTRA - 6), (0, 0)))
+    resp_side = by_head(resp_kv[0, 0], bias)
+    me = lax.axis_index("resp")
+    y, x = me // sizes[1], me % sizes[1]
+    ids = [(y + dy) % sizes[0] * sizes[1] + (x + dx) % sizes[1] for dy, dx in PLACES]
+    meta = jnp.concatenate([prompt_len, resp_len[0], jnp.stack(ids)]).astype(jnp.int32)
+    sources = (meta, queries, cotangent, resp_side)
+    outs, first_resp, parts = attend(*sources, pieces, *CALLS[0], (term,), ())
+    parts = lax.all_to_all(parts, "resp", 0, 0)
+    (attn_out, d_q), last_resp, held = attend(*sources, pieces, *CALLS[1], (), outs)
+    first_grad, term, held = relay(parts, held)
+    arrived = lax.all_to_all(held, "resp", 0, 0)
+    for step in TAIL_STEPS:
+        term = exchange_sum(term, "prompt", step)
+    d_bias = term.reshape(KVH * HD) / (members * prompts)
+    last_grad = jnp.sum(arrived.astype(jnp.float32), axis=0)
+    prompt_grad = jnp.concatenate([first_grad, last_grad]).astype(jnp.bfloat16)
     return (
         attn_out[None, None],
         d_q[None, None],
-        by_pair(jnp.concatenate(resp_grads))[None, None],
-        by_pair(jnp.concatenate(prompt_grads))[None],
+        by_pair(jnp.concatenate([first_resp, last_resp]))[None, None],
+        by_pair(prompt_grad)[None],
         d_bias,
     )
 

time: 133 us -> 89.5 us (0.67)
  blocking collectives: 19.7 us -> 0 us
  waiting for transfers between devices: 31.1 us -> 13.2 us
  local copies, waits for them, and re-layouts: 15 us -> 6.62 us
  Pallas kernels: 28 us -> 30.7 us
  other arithmetic: 2.9 us -> 1.1 us
    all_to_all x1 -> x0, blocking collectives: 19.7 us -> none  [shards(): arrived = lax.all_to_all(part, 'resp', 0, 0)]
    all_to_all x3 -> x2, waiting for transfers between devices: 14.4 us -> 0.01 us  [the longest x1 0.01 us: shards(): arrived = lax.all_to_all(held, 'resp', 0, 0)]
    ppermute x8 -> x12, starting transfers between devices: 18.7 us -> 23.1 us  [the longest x5 15.5 us: exchange_sum(): return term + lax.ppermute(term, axis, [(i, i ^ step) for i in range(size)])]
    unnamed x20 -> x29, local copies, waits for them, and re-layouts: 6.14 us -> 2.33 us
    ppermute x8 -> x12, waiting for transfers between devices: 16.7 us -> 13.2 us  [the longest x7 9.82 us: move(): lax.ppermute(value, 'resp', [(y * nx + x, (y + dy) % ny * nx + (x + dx) %...]
    convert_element_type x2, local copies, waits for them, and re-layouts: 3.5 us -> 0.35 us  [by_head(): biased = pairs.astype(jnp.float32) + jnp.stack([jnp.zeros_like(bias), bias])]
    all_to_all x3 -> x2, starting transfers between devices: 15.4 us -> 12.3 us  [the longest x1 6.38 us: shards(): parts = lax.all_to_all(parts, 'resp', 0, 0)]
    pallas_call x2 -> x3, Pallas kernels: 28 us -> 30.7 us  [the longest x2 29.9 us: attend(): pl.pallas_call(functools.partial(attend_body, slots, rows, shard, len(ter...]
  transfers between devices with their start and end apart: 11 -> 14, of which waited for: 9 -> 6; matrix products, arithmetic and copies ran while one was open for 6% -> 4% of each run, Pallas kernels for 11% -> 17%
where the time goes in v2:
time: 89.5 us; the launch traced here: 89.2 us
  starting transfers between devices  35.3 us (39%)
  Pallas kernels  30.7 us (34%)
  waiting for transfers between devices  13.2 us (15%)
  local copies, waits for them, and re-layouts  6.62 us (7%)
  between operations  2.23 us (2%)
  other arithmetic  1.1 us (1%)
    pallas_call x2, Pallas kernels, attend(): pl.pallas_call(functools.partial(attend_body, slots, rows, shard, len(ter...  29.9 us
    ppermute x5, starting transfers between devices, exchange_sum(): return term + lax.ppermute(term, axis, [(i, i ^ step) for i in range(size)])  15.5 us
    ppermute x7, waiting for transfers between devices, move(): lax.ppermute(value, 'resp', [(y * nx + x, (y + dy) % ny * nx + (x + dx) %...  9.82 us
    ppermute x7, starting transfers between devices, move(): lax.ppermute(value, 'resp', [(y * nx + x, (y + dy) % ny * nx + (x + dx) %...  7.51 us
    all_to_all x1, starting transfers between devices, shards(): parts = lax.all_to_all(parts, 'resp', 0, 0)  6.38 us
    all_to_all x1, starting transfers between devices, shards(): arrived = lax.all_to_all(held, 'resp', 0, 0)  5.88 us
    ppermute x5, waiting for transfers between devices, exchange_sum(): return term + lax.ppermute(term, axis, [(i, i ^ step) for i in range(size)])  3.37 us
    unnamed x29, local copies, waits for them, and re-layouts  2.33 us
  transfers between devices with their start and end apart: 14, of which 6 were waited for; matrix products, arithmetic and copies ran while one was open for 4% of the time, Pallas kernels for 17%

profile of v2, /device:TPU:2, one launch (start us, length us, event | category | flops | bytes accessed | tf_op | source)
XLA Modules:
  0.0 89.2 jit_solution(13950473589827166198)
XLA Ops:
  0.6 0.8 stack.53
  1.5 1.1 %copy.30 = bf16[1,128,2,512]{1,3,2,0:T(8,128)(2,1)S(1)} copy(bf16[1,128,2,512]{3,2,1,0:T(2,128)(2,1)} %param.9) | data formatting | bytes 524288 | tf_op args[2]
  2.8 2.3 %collective-permute-start.2 = (bf16[4,128,256]{2,1,0:T(8,128)(2,1)S(1)}, bf16[4,128,256]{2,1,0:T(8,128)(2,1)S(1)}, u32[]{:S(2)}, u32[]{:S(2)}) collective-permute-start(bf16[4,128,256]{2,1,0:T(8,128)(2,1)S(1)} %copy_bitcast_fusion.1.refs_0_), channel_id=1, source_target_pairs={{0,96},{32,0},{64,32},{96,64},{128,224},{160,128},{192,160},{224,1... | collective-permute-start | bytes 786440 | tf_op jit(solution)/shard_map/ppermute | solution.py:224
  5.2 1.3 %collective-permute-start = (bf16[4,128,256]{2,1,0:T(8,128)(2,1)S(1)}, bf16[4,128,256]{2,1,0:T(8,128)(2,1)S(1)}, u32[]{:S(2)}, u32[]{:S(2)}) collective-permute-start(bf16[4,128,256]{2,1,0:T(8,128)(2,1)S(1)} %copy_bitcast_fusion.1.refs_0_), channel_id=1, source_target_pairs={{0,128},{32,160},{64,192},{96,224},{128,0},{160,32},{192,64},{224,... | collective-permute-start | bytes 786440 | tf_op jit(solution)/shard_map/ppermute | solution.py:224
  7.2 0.3 select_reduce_fusion
  7.6 3.4 %collective-permute-start.7 = (f32[4,128]{1,0:T(4,128)S(1)}, f32[4,128]{1,0:T(4,128)S(1)}, u32[]{:S(2)}, u32[]{:S(2)}) collective-permute-start(f32[4,128]{1,0:T(4,128)S(1)} %reduce_sum.28), channel_id=1, source_target_pairs={{0,4},{1,5},{2,6},{3,7},{4,0},{5,1},{6,2},{7,3},{8,12},{9,13},{10,... | collective-permute-start | bytes 6152 | tf_op jit(solution)/shard_map/ppermute | solution.py:244
  10.9 0.5 copy.27
  11.5 0.2 copy.28
  11.7 0.8 collective-permute-start.4
  12.5 1.5 %collective-permute-start.3 = (bf16[4,128,256]{2,1,0:T(8,128)(2,1)S(1)}, bf16[4,128,256]{2,1,0:T(8,128)(2,1)S(1)}, u32[]{:S(2)}, u32[]{:S(2)}) collective-permute-start(bf16[4,128,256]{2,1,0:T(8,128)(2,1)S(1)} %collective-permute-done.refs_1_), channel_id=1, source_target_pairs={{0,32},{32,64},{64,96},{96,0},{128,160},{160,192},{192,224},{224,1... | collective-permute-start | bytes 786440 | tf_op jit(solution)/shard_map/ppermute | solution.py:224
  14.1 0.6 collective-permute-start.5
  14.8 4.0 %collective-permute-done.4.refs_5_ = bf16[4,128,256]{2,1,0:T(8,128)(2,1)S(1)} collective-permute-done((bf16[4,128,256]{2,1,0:T(8,128)(2,1)S(1)}, bf16[4,128,256]{2,1,0:T(8,128)(2,1)S(1)}, u32[]{:S(2)}, u32[]{:S(2)}) %collective-permute-start.4) | collective-permute-done | bytes 262176 | tf_op jit(solution)/shard_map/ppermute | solution.py:224
  18.7 0.7 collective-permute-done.3.refs_4_
  19.5 3.0 %collective-permute-start.8 = (f32[4,128]{1,0:T(4,128)S(1)}, f32[4,128]{1,0:T(4,128)S(1)}, u32[]{:S(2)}, u32[]{:S(2)}) collective-permute-start(f32[4,128]{1,0:T(4,128)S(1)} %add_add_fusion), channel_id=1, source_target_pairs={{0,16},{1,17},{2,18},{3,19},{4,20},{5,21},{6,22},{7,23},{8,24},{9,... | collective-permute-start | bytes 6152 | tf_op jit(solution)/shard_map/ppermute | solution.py:244
  23.2 0.9 %collective-permute-start.6 = (bf16[4,128,256]{2,1,0:T(8,128)(2,1)S(1)}, bf16[4,128,256]{2,1,0:T(8,128)(2,1)S(1)}, u32[]{:S(2)}, u32[]{:S(2)}) collective-permute-start(bf16[4,128,256]{2,1,0:T(8,128)(2,1)S(1)} %collective-permute-done.5.refs_6_), channel_id=1, source_target_pairs={{0,128},{32,160},{64,192},{96,224},{128,0},{160,32},{192,64},{224,... | collective-permute-start | bytes 786440 | tf_op jit(solution)/shard_map/ppermute | solution.py:224
  24.1 0.5 collective-permute-done.8
  24.7 5.1 %collective-permute-done.6.refs_7_ = bf16[4,128,256]{2,1,0:T(8,128)(2,1)S(1)} collective-permute-done((bf16[4,128,256]{2,1,0:T(8,128)(2,1)S(1)}, bf16[4,128,256]{2,1,0:T(8,128)(2,1)S(1)}, u32[]{:S(2)}, u32[]{:S(2)}) %collective-permute-start.6) | collective-permute-done | bytes 262176 | tf_op jit(solution)/shard_map/ppermute | solution.py:224
  29.8 14.8 %attend.2 = (bf16[256,2560]{1,0:T(8,128)(2,1)}, bf16[256,2560]{1,0:T(8,128)(2,1)}, bf16[2,256,256]{2,1,0:T(8,128)(2,1)S(1)}, bf16[8,2,144,256]{3,2,1,0:T(8,128)(2,1)}) custom-call(s32[10]{0:T(128)S(1)} %concatenate.15.meta, bf16[256,2560]{1,0:T(8,128)(2,1)} %bitcast.55, bf16[256,2560]{1,0:T(8,128)(2,1)} %bitcast.50, ...), custom_call_target="tpu_custom_call" | custom-call | flops 5033164800 | bytes 2621440 | tf_op jit(solution)/shard_map/attend/pallas_call | solution.py:164
  44.8 6.4 %all-to-all-start = ((bf16[8,2,144,256]{3,2,1,0:T(8,128)(2,1)}), bf16[8,2,144,256]{3,2,1,0:T(8,128)(2,1)S(1)}, u32[]{:S(2)}, u32[]{:S(2)}) async-start(bf16[8,2,144,256]{3,2,1,0:T(8,128)(2,1)} %get-tuple-element.22), calls=%async_computation | async-start | bytes 2359296 | tf_op jit(solution)/shard_map/all_to_all | solution.py:277
  51.1 15.0 %attend.3 = (bf16[256,2560]{1,0:T(8,128)(2,1)}, bf16[256,2560]{1,0:T(8,128)(2,1)}, bf16[2,256,256]{2,1,0:T(8,128)(2,1)S(1)}, bf16[8,2,128,256]{3,2,1,0:T(8,128)(2,1)}) custom-call(s32[10]{0:T(128)S(1)} %concatenate.15.meta, bf16[256,2560]{1,0:T(8,128)(2,1)} %bitcast.56, bf16[256,2560]{1,0:T(8,128)(2,1)} %bitcast.51, ...), custom_call_target="tpu_custom_call", output_to_operand_aliasing={{0}: (12, {}), {1}: (13, {})} | custom-call | flops 5033164800 | bytes 2621440 | tf_op jit(solution)/shard_map/attend/pallas_call | solution.py:164
  66.2 0.8 relay.1
  67.0 5.9 %all-to-all-start.1 = ((bf16[8,2,128,256]{3,2,1,0:T(8,128)(2,1)}), bf16[8,2,128,256]{3,2,1,0:T(8,128)(2,1)S(1)}, u32[]{:S(2)}, u32[]{:S(2)}) async-start(bf16[8,2,128,256]{3,2,1,0:T(8,128)(2,1)} %get-tuple-element.25), calls=%async_computation.1 | async-start | bytes 2097152 | tf_op jit(solution)/shard_map/all_to_all | solution.py:280
  72.9 1.1 %collective-permute-done.9 = f32[2,256]{1,0:T(2,128)S(1)} collective-permute-done((f32[2,256]{1,0:T(2,128)S(1)}, f32[2,256]{1,0:T(2,128)S(1)}, u32[]{:S(2)}, u32[]{:S(2)}) %collective-permute-start.9) | collective-permute-done | bytes 2080 | tf_op jit(solution)/shard_map/ppermute | solution.py:244
  74.1 1.9 %collective-permute-start.10 = (f32[2,256]{1,0:T(2,128)S(1)}, f32[2,256]{1,0:T(2,128)S(1)}, u32[]{:S(2)}, u32[]{:S(2)}) collective-permute-start(f32[2,256]{1,0:T(2,128)S(1)} %add.160), channel_id=1, source_target_pairs={{0,2},{1,3},{2,0},{3,1},{4,6},{5,7},{6,4},{7,5},{8,10},{9,11},{10,... | collective-permute-start | bytes 6152 | tf_op jit(solution)/shard_map/ppermute | solution.py:244
  76.0 1.7 %collective-permute-done.10 = f32[2,256]{1,0:T(2,128)S(1)} collective-permute-done((f32[2,256]{1,0:T(2,128)S(1)}, f32[2,256]{1,0:T(2,128)S(1)}, u32[]{:S(2)}, u32[]{:S(2)}) %collective-permute-start.10) | collective-permute-done | bytes 2080 | tf_op jit(solution)/shard_map/ppermute | solution.py:244
  77.7 7.3 %collective-permute-start.11 = (f32[2,256]{1,0:T(2,128)S(1)}, f32[2,256]{1,0:T(2,128)S(1)}, u32[]{:S(2)}, u32[]{:S(2)}) collective-permute-start(f32[2,256]{1,0:T(2,128)S(1)} %add.161), channel_id=1, source_target_pairs={{0,8},{1,9},{2,10},{3,11},{4,12},{5,13},{6,14},{7,15},{8,0},{9,1},... | collective-permute-start | bytes 6152 | tf_op jit(solution)/shard_map/ppermute | solution.py:244
  85.1 0.7 copy.33
  85.8 1.0 %broadcast_in_dim_reshape.6 = bf16[1,1,256,2,512]{4,3,2,1,0:T(2,128)(2,1)} reshape(bf16[256,2,4,128]{3,2,1,0:T(4,128)(2,1)S(1)} %copy.33) | data formatting | bytes 1048576 | tf_op jit(solution)/shard_map/broadcast_in_dim;reshape | solution.py:289
  86.9 0.6 copy.37
  87.7 0.3 maximum_bitcast_fusion
  88.0 0.3 copy.34
  88.4 0.8 broadcast_in_dim_reshape.7
  (59 shorter events, 1.0 us)
Async XLA Ops:
  0.6 6.5 %copy-start.9 = (bf16[1,1,256,2560]{3,2,1,0:T(8,128)(2,1)S(1)}, bf16[1,1,256,2560]{3,2,1,0:T(8,128)(2,1)}, u32[]{:S(2)}) copy-start(bf16[1,1,256,2560]{3,2,1,0:T(8,128)(2,1)} %param.13) | copy-start | bytes 3932164
  2.8 8.2 %copy-start.10 = (bf16[1,1,256,2,512]{4,3,2,1,0:T(2,128)(2,1)S(1)}, bf16[1,1,256,2,512]{4,3,2,1,0:T(2,128)(2,1)}, u32[]{:S(2)}) copy-start(bf16[1,1,256,2,512]{4,3,2,1,0:T(2,128)(2,1)} %param.8) | copy-start | bytes 1572868
  2.8 27.0 %copy-start.1 = (bf16[4,128,256]{2,1,0:T(8,128)(2,1)}, bf16[4,128,256]{2,1,0:T(8,128)(2,1)S(1)}, u32[]{:S(2)}) copy-start(bf16[4,128,256]{2,1,0:T(8,128)(2,1)S(1)} %copy_bitcast_fusion.1.refs_0_) | copy-start | bytes 786436
  2.8 8.8 %collective-permute-start.2 = (bf16[4,128,256]{2,1,0:T(8,128)(2,1)S(1)}, bf16[4,128,256]{2,1,0:T(8,128)(2,1)S(1)}, u32[]{:S(2)}, u32[]{:S(2)}) collective-permute-start(bf16[4,128,256]{2,1,0:T(8,128)(2,1)S(1)} %copy_bitcast_fusion.1.refs_0_), channel_id=1, source_target_pairs={{0,96},{32,0},{64,32},{96,64},{128,224},{160,128},{192,160},{224,1... | collective-permute-start | bytes 786440 | tf_op jit(solution)/shard_map/ppermute | solution.py:224
  5.2 19.5 %collective-permute-start.1 = (bf16[4,128,256]{2,1,0:T(8,128)(2,1)S(1)}, bf16[4,128,256]{2,1,0:T(8,128)(2,1)S(1)}, u32[]{:S(2)}, u32[]{:S(2)}) collective-permute-start(bf16[4,128,256]{2,1,0:T(8,128)(2,1)S(1)} %copy_bitcast_fusion.1.refs_0_), channel_id=1, source_target_pairs={{0,32},{32,64},{64,96},{96,0},{128,160},{160,192},{192,224},{224,1... | collective-permute-start | bytes 786440 | tf_op jit(solution)/shard_map/ppermute | solution.py:224
  5.2 7.4 %collective-permute-start = (bf16[4,128,256]{2,1,0:T(8,128)(2,1)S(1)}, bf16[4,128,256]{2,1,0:T(8,128)(2,1)S(1)}, u32[]{:S(2)}, u32[]{:S(2)}) collective-permute-start(bf16[4,128,256]{2,1,0:T(8,128)(2,1)S(1)} %copy_bitcast_fusion.1.refs_0_), channel_id=1, source_target_pairs={{0,128},{32,160},{64,192},{96,224},{128,0},{160,32},{192,64},{224,... | collective-permute-start | bytes 786440 | tf_op jit(solution)/shard_map/ppermute | solution.py:224
  7.6 11.9 %collective-permute-start.7 = (f32[4,128]{1,0:T(4,128)S(1)}, f32[4,128]{1,0:T(4,128)S(1)}, u32[]{:S(2)}, u32[]{:S(2)}) collective-permute-start(f32[4,128]{1,0:T(4,128)S(1)} %reduce_sum.28), channel_id=1, source_target_pairs={{0,4},{1,5},{2,6},{3,7},{4,0},{5,1},{6,2},{7,3},{8,12},{9,13},{10,... | collective-permute-start | bytes 6152 | tf_op jit(solution)/shard_map/ppermute | solution.py:244
  11.7 33.0 %copy-start.2 = (bf16[4,128,256]{2,1,0:T(8,128)(2,1)}, bf16[4,128,256]{2,1,0:T(8,128)(2,1)S(1)}, u32[]{:S(2)}) copy-start(bf16[4,128,256]{2,1,0:T(8,128)(2,1)S(1)} %collective-permute-done.2.refs_3_) | copy-start | bytes 786436
  11.7 7.0 %collective-permute-start.4 = (bf16[4,128,256]{2,1,0:T(8,128)(2,1)S(1)}, bf16[4,128,256]{2,1,0:T(8,128)(2,1)S(1)}, u32[]{:S(2)}, u32[]{:S(2)}) collective-permute-start(bf16[4,128,256]{2,1,0:T(8,128)(2,1)S(1)} %collective-permute-done.2.refs_3_), channel_id=1, source_target_pairs={{0,128},{32,160},{64,192},{96,224},{128,0},{160,32},{192,64},{224,... | collective-permute-start | bytes 786440 | tf_op jit(solution)/shard_map/ppermute | solution.py:224
  12.5 32.2 %copy-start.4 = (bf16[4,128,256]{2,1,0:T(8,128)(2,1)}, bf16[4,128,256]{2,1,0:T(8,128)(2,1)S(1)}, u32[]{:S(2)}) copy-start(bf16[4,128,256]{2,1,0:T(8,128)(2,1)S(1)} %collective-permute-done.refs_1_) | copy-start | bytes 786436
  12.5 6.9 %collective-permute-start.3 = (bf16[4,128,256]{2,1,0:T(8,128)(2,1)S(1)}, bf16[4,128,256]{2,1,0:T(8,128)(2,1)S(1)}, u32[]{:S(2)}, u32[]{:S(2)}) collective-permute-start(bf16[4,128,256]{2,1,0:T(8,128)(2,1)S(1)} %collective-permute-done.refs_1_), channel_id=1, source_target_pairs={{0,32},{32,64},{64,96},{96,0},{128,160},{160,192},{192,224},{224,1... | collective-permute-start | bytes 786440 | tf_op jit(solution)/shard_map/ppermute | solution.py:224
  14.1 30.6 %copy-start = (bf16[4,256,256]{2,1,0:T(8,128)(2,1)}, bf16[4,256,256]{2,1,0:T(8,128)(2,1)S(1)}, u32[]{:S(2)}) copy-start(bf16[4,256,256]{2,1,0:T(8,128)(2,1)S(1)} %copy_bitcast_fusion.kvr_ref) | copy-start | bytes 1572868
  14.1 9.0 %collective-permute-start.5 = (bf16[4,128,256]{2,1,0:T(8,128)(2,1)S(1)}, bf16[4,128,256]{2,1,0:T(8,128)(2,1)S(1)}, u32[]{:S(2)}, u32[]{:S(2)}) collective-permute-start(bf16[4,128,256]{2,1,0:T(8,128)(2,1)S(1)} %collective-permute-done.2.refs_3_), channel_id=1, source_target_pairs={{0,96},{32,0},{64,32},{96,64},{128,224},{160,128},{192,160},{224,1... | collective-permute-start | bytes 786440 | tf_op jit(solution)/shard_map/ppermute | solution.py:224
  18.7 26.0 %copy-start.5 = (bf16[4,128,256]{2,1,0:T(8,128)(2,1)}, bf16[4,128,256]{2,1,0:T(8,128)(2,1)S(1)}, u32[]{:S(2)}) copy-start(bf16[4,128,256]{2,1,0:T(8,128)(2,1)S(1)} %collective-permute-done.4.refs_5_) | copy-start | bytes 786436
  19.4 25.3 %copy-start.6 = (bf16[4,128,256]{2,1,0:T(8,128)(2,1)}, bf16[4,128,256]{2,1,0:T(8,128)(2,1)S(1)}, u32[]{:S(2)}) copy-start(bf16[4,128,256]{2,1,0:T(8,128)(2,1)S(1)} %collective-permute-done.3.refs_4_) | copy-start | bytes 786436
  19.5 5.2 %collective-permute-start.8 = (f32[4,128]{1,0:T(4,128)S(1)}, f32[4,128]{1,0:T(4,128)S(1)}, u32[]{:S(2)}, u32[]{:S(2)}) collective-permute-start(f32[4,128]{1,0:T(4,128)S(1)} %add_add_fusion), channel_id=1, source_target_pairs={{0,16},{1,17},{2,18},{3,19},{4,20},{5,21},{6,22},{7,23},{8,24},{9,... | collective-permute-start | bytes 6152 | tf_op jit(solution)/shard_map/ppermute | solution.py:244
  23.2 21.5 %copy-start.7 = (bf16[4,128,256]{2,1,0:T(8,128)(2,1)}, bf16[4,128,256]{2,1,0:T(8,128)(2,1)S(1)}, u32[]{:S(2)}) copy-start(bf16[4,128,256]{2,1,0:T(8,128)(2,1)S(1)} %collective-permute-done.5.refs_6_) | copy-start | bytes 786436
  23.2 6.6 %collective-permute-start.6 = (bf16[4,128,256]{2,1,0:T(8,128)(2,1)S(1)}, bf16[4,128,256]{2,1,0:T(8,128)(2,1)S(1)}, u32[]{:S(2)}, u32[]{:S(2)}) collective-permute-start(bf16[4,128,256]{2,1,0:T(8,128)(2,1)S(1)} %collective-permute-done.5.refs_6_), channel_id=1, source_target_pairs={{0,128},{32,160},{64,192},{96,224},{128,0},{160,32},{192,64},{224,... | collective-permute-start | bytes 786440 | tf_op jit(solution)/shard_map/ppermute | solution.py:224
  24.7 20.1 %copy-start.3 = (bf16[4,128,256]{2,1,0:T(8,128)(2,1)}, bf16[4,128,256]{2,1,0:T(8,128)(2,1)S(1)}, u32[]{:S(2)}) copy-start(bf16[4,128,256]{2,1,0:T(8,128)(2,1)S(1)} %collective-permute-done.1.refs_2_) | copy-start | bytes 786436
  29.8 14.9 %copy-start.8 = (bf16[4,128,256]{2,1,0:T(8,128)(2,1)}, bf16[4,128,256]{2,1,0:T(8,128)(2,1)S(1)}, u32[]{:S(2)}) copy-start(bf16[4,128,256]{2,1,0:T(8,128)(2,1)S(1)} %collective-permute-done.6.refs_7_) | copy-start | bytes 786436
  44.8 21.4 %all-to-all-start = ((bf16[8,2,144,256]{3,2,1,0:T(8,128)(2,1)}), bf16[8,2,144,256]{3,2,1,0:T(8,128)(2,1)S(1)}, u32[]{:S(2)}, u32[]{:S(2)}) async-start(bf16[8,2,144,256]{3,2,1,0:T(8,128)(2,1)} %get-tuple-element.22), calls=%async_computation | async-start | bytes 2359296 | tf_op jit(solution)/shard_map/all_to_all | solution.py:277
  67.0 5.9 %copy-start.12 = (f32[2,256]{1,0:T(2,128)S(1)}, f32[2,256]{1,0:T(2,128)}, u32[]{:S(2)}) copy-start(f32[2,256]{1,0:T(2,128)} %get-tuple-element.26) | copy-start | bytes 6148
  67.0 20.5 %all-to-all-start.1 = ((bf16[8,2,128,256]{3,2,1,0:T(8,128)(2,1)}), bf16[8,2,128,256]{3,2,1,0:T(8,128)(2,1)S(1)}, u32[]{:S(2)}, u32[]{:S(2)}) async-start(bf16[8,2,128,256]{3,2,1,0:T(8,128)(2,1)} %get-tuple-element.25), calls=%async_computation.1 | async-start | bytes 2097152 | tf_op jit(solution)/shard_map/all_to_all | solution.py:280
  72.9 1.2 %collective-permute-start.9 = (f32[2,256]{1,0:T(2,128)S(1)}, f32[2,256]{1,0:T(2,128)S(1)}, u32[]{:S(2)}, u32[]{:S(2)}) collective-permute-start(f32[2,256]{1,0:T(2,128)S(1)} %copy-done.12), channel_id=1, source_target_pairs={{0,1},{1,0},{2,3},{3,2},{4,5},{5,4},{6,7},{7,6},{8,9},{9,8},{10,11... | collective-permute-start | bytes 6152 | tf_op jit(solution)/shard_map/ppermute | solution.py:244
  74.1 3.6 %collective-permute-start.10 = (f32[2,256]{1,0:T(2,128)S(1)}, f32[2,256]{1,0:T(2,128)S(1)}, u32[]{:S(2)}, u32[]{:S(2)}) collective-permute-start(f32[2,256]{1,0:T(2,128)S(1)} %add.160), channel_id=1, source_target_pairs={{0,2},{1,3},{2,0},{3,1},{4,6},{5,7},{6,4},{7,5},{8,10},{9,11},{10,... | collective-permute-start | bytes 6152 | tf_op jit(solution)/shard_map/ppermute | solution.py:244
  77.7 9.2 %collective-permute-start.11 = (f32[2,256]{1,0:T(2,128)S(1)}, f32[2,256]{1,0:T(2,128)S(1)}, u32[]{:S(2)}, u32[]{:S(2)}) collective-permute-start(f32[2,256]{1,0:T(2,128)S(1)} %add.161), channel_id=1, source_target_pairs={{0,8},{1,9},{2,10},{3,11},{4,12},{5,13},{6,14},{7,15},{8,0},{9,1},... | collective-permute-start | bytes 6152 | tf_op jit(solution)/shard_map/ppermute | solution.py:244
  85.1 1.7 %copy-start.11 = (f32[2,128,256]{2,1,0:T(8,128)S(1)}, f32[2,128,256]{2,1,0:T(8,128)}, u32[]{:S(2)}) copy-start(f32[2,128,256]{2,1,0:T(8,128)} %get-tuple-element.24) | copy-start | bytes 786436

commit v3 on v2

--- a/solution.py
+++ b/solution.py
@@ -17,7 +17,7 @@
 LOG2E = math.log2(math.e)
 CALLS = ((0, 2), (2, 2))
 EXTRA = 16
-HEAD_STEPS, TAIL_STEPS = (4, 16), (1, 2, 8)
+HEAD_STEPS, TAIL_STEPS = (16, 4), (1, 2, 8)
 
 
 def dot(a, b):
@@ -31,7 +31,7 @@
     refs = refs[chained:]
     ao_ref, dq_ref, dkvr_ref, parts_ref = refs[:4]
     refs = refs[4:]
-    k_scr, v_scr, kt_scr, vt_scr, s_scr, p_scr, ds_scr, q_scr, dol_scr = refs
+    k_scr, v_scr, kt_scr, vt_scr, s_scr, p_scr, ds_scr, qt_scr, dol_scr, dk_scr, dv_scr = refs
     prompt = slots * shard
     plen, rlen = meta[0], meta[1]
     kvr = kvr_ref[0]
@@ -63,58 +63,96 @@
         lax.broadcasted_iota(jnp.int32, (16, rows), 0) == 0, 1.0, 0.0
     ).astype(jnp.bfloat16)
     live = lax.broadcasted_iota(jnp.int32, (1, rows), 1) < rlen
-    maxes = {}
-
-    def scores(h):
-        q = q_ref[:, h * HD : (h + 1) * HD]
-        q_scr[h * rows : (h + 1) * rows, :] = q
-        s = lax.dot_general(k_scr[...], q, NT, preferred_element_type=jnp.float32)
-        sp = s[:prompt]
-        causal = lax.broadcasted_iota(jnp.int32, (rows, rows), 0) <= lax.broadcasted_iota(
-            jnp.int32, (rows, rows), 1
+    causal = lax.broadcasted_iota(jnp.int32, (rows, rows), 0) <= lax.broadcasted_iota(
+        jnp.int32, (rows, rows), 1
+    )
+    blocks = [slice(c, c + rows) for c in range(0, prompt + rows, rows)]
+    maxes, outs, dots, dqs = {}, {}, {}, {}
+
+    def head(h):
+        return slice(h * rows, (h + 1) * rows)
+
+    def lanes(h):
+        return slice(h * HD, (h + 1) * HD)
+
+    def scores(h, b):
+        at = blocks[b]
+        if b == 0:
+            qt_scr[:, head(h)] = q_ref[:, lanes(h)].astype(jnp.float32).T.astype(jnp.bfloat16)
+        s = dot(k_scr[at, :], qt_scr[:, head(h)])
+        if at.start >= prompt:
+            s = jnp.where(causal, s, NEG)
+        s_scr[h % 2, at, :] = s
+        m = jnp.max(s.reshape(rows // 8, 8, rows), axis=0)
+        maxes[h] = m if b == 0 else jnp.maximum(maxes[h], m)
+        if b == len(blocks) - 1:
+            maxes[h] = jnp.max(maxes[h], axis=0, keepdims=True)
+
+    def exponentials(h, b):
+        at = blocks[b]
+        e = jnp.exp2((s_scr[h % 2, at, :] - maxes[h]) * (SCALE * LOG2E))
+        p_scr[at, head(h)] = e.astype(jnp.bfloat16)
+
+    def outputs(h, b):
+        at = blocks[b]
+        o = dot(vt_scr[:, at], p_scr[at, head(h)])
+        outs[h] = o if b == 0 else outs[h] + o
+
+    def score_grads(h, b):
+        at = blocks[b]
+        if b == 0:
+            share = jnp.where(live, 1.0 / outs[h][HD : HD + 1], 0.0)
+            normal = outs[h][:HD] * share
+            ao_ref[:, lanes(h)] = normal.T.astype(jnp.bfloat16)
+            dol = do_ref[:, lanes(h)].astype(jnp.float32).T * share
+            row_dot = jnp.sum(dol * normal, axis=0, keepdims=True)
+            dol_scr[head(h), :] = dol.T.astype(jnp.bfloat16)
+            dots[h] = dol.astype(jnp.bfloat16), row_dot
+        dol, row_dot = dots[h]
+        dp = dot(v_scr[at, :], dol)
+        ds_scr[at, head(h)] = p_scr[at, head(h)] * (dp - row_dot).astype(jnp.bfloat16)
+
+    def query_grads(h, b):
+        at = blocks[b]
+        d = dot(kt_scr[:, at], ds_scr[at, head(h)])
+        dqs[h] = d if b == 0 else dqs[h] + d
+        if b == len(blocks) - 1:
+            dq_ref[:, lanes(h)] = (dqs[h] * SCALE).T.astype(jnp.bfloat16)
+
+    def key_grads(h, b):
+        at = blocks[b]
+        d = lax.dot_general(
+            qt_scr[:, head(h)], ds_scr[at, head(h)], NT, preferred_element_type=jnp.float32
         )
-        sr = jnp.where(causal, s[prompt:], NEG)
-        s_scr[h % 2, :prompt, :] = sp
-        s_scr[h % 2, prompt:, :] = sr
-        maxes[h] = jnp.maximum(
-            jnp.max(sp, axis=0, keepdims=True), jnp.max(sr, axis=0, keepdims=True)
-        )
-
-    def exponentials(h):
-        e = jnp.exp2((s_scr[h % 2] - maxes[h]) * (SCALE * LOG2E))
-        p_scr[:, h * rows : (h + 1) * rows] = e.astype(jnp.bfloat16)
-
-    def outputs(h):
-        at = slice(h * rows, (h + 1) * rows)
-        lanes = slice(h * HD, (h + 1) * HD)
-        p = p_scr[:, at]
-        ot = dot(vt_scr[...], p)
-        share = jnp.where(live, 1.0 / ot[HD : HD + 1], 0.0)
-        normal = ot[:HD] * share
-        ao_ref[:, lanes] = normal.T.astype(jnp.bfloat16)
-        dol = do_ref[:, lanes].astype(jnp.float32).T * share
-        row_dot = jnp.sum(dol * normal, axis=0, keepdims=True)
-        dol_scr[at, :] = dol.T.astype(jnp.bfloat16)
-        dp = dot(v_scr[...], dol.astype(jnp.bfloat16))
-        ds_scr[:, at] = p * (dp - row_dot).astype(jnp.bfloat16)
-
-    def query_grads(h):
-        at = slice(h * rows, (h + 1) * rows)
-        dqt = dot(kt_scr[...], ds_scr[:, at]) * SCALE
-        dq_ref[:, h * HD : (h + 1) * HD] = dqt.T.astype(jnp.bfloat16)
-
-    stages = (scores, exponentials, outputs, query_grads)
-    for t in range(GROUP + len(stages) - 1):
-        for lag, stage in enumerate(stages):
-            if 0 <= t - lag < GROUP:
-                stage(t - lag)
-    dk = dot(ds_scr[...], q_scr[...]) * SCALE
-    dv = dot(p_scr[...], dol_scr[...])
+        dk_scr[:, at] = d if h == 0 else dk_scr[:, at] + d
+
+    def value_grads(h, b):
+        at = blocks[b]
+        d = dot(p_scr[at, head(h)], dol_scr[head(h), :])
+        dv_scr[at, :] = d if h == 0 else dv_scr[at, :] + d
+
+    stages = ((query_grads, 4), (score_grads, 3), (outputs, 2), (exponentials, 1), (scores, 0))
+    stages += ((key_grads, 4), (value_grads, 4))
+    for t in range(GROUP + 4):
+        for b in range(len(blocks)):
+            for stage, lag in stages:
+                if 0 <= t - lag < GROUP:
+                    stage(t - lag, b)
+    dk = (dk_scr[...] * SCALE).T
+    dv = dv_scr[...]
+    if term:
+        rest, split = term_ref[...], []
+        for _ in range(3):
+            split.append(rest.astype(jnp.bfloat16).astype(jnp.float32))
+            rest = rest - split[-1]
+        split.append(jnp.zeros_like(rest))
+        extras = jnp.concatenate(split, axis=0).astype(jnp.bfloat16)
     for s in range(slots):
         at = slice(s * shard, (s + 1) * shard)
         out = parts_ref.at[meta[2 + s], 0]
         if term:
-            out[shard:, :] = term_ref[...]
+            out[shard:, :HD] = extras
+            out[shard:, HD:] = jnp.zeros_like(extras)
         out[:shard, :HD] = jnp.where(seen[s], dk[at], 0.0).astype(jnp.bfloat16)
         out[:shard, HD:] = jnp.where(seen[s], dv[at], 0.0).astype(jnp.bfloat16)
     dkvr_ref[0, :, :HD] = dk[prompt:].astype(jnp.bfloat16)
@@ -134,7 +172,7 @@
     whole = pl.BlockSpec(memory_space=pl.ANY)
     head = pl.BlockSpec((rows, wide), lambda g, m: (0, first + g))
     piece = pl.BlockSpec((1, shard, 2 * HD), lambda g, m: (first + g, 0, 0))
-    part = (slots, count, shard + sum(t.shape[0] for t in term), 2 * HD)
+    part = (slots, count, shard + EXTRA * len(term), 2 * HD)
     grid_spec = pltpu.PrefetchScalarGridSpec(
         num_scalar_prefetch=1,
         grid=(count,),
@@ -156,8 +194,10 @@
             pltpu.VMEM((2, cols, rows), jnp.float32),
             pltpu.VMEM((cols, GROUP * rows), bf),
             pltpu.VMEM((cols, GROUP * rows), bf),
+            pltpu.VMEM((HD, GROUP * rows), bf),
             pltpu.VMEM((GROUP * rows, HD), bf),
-            pltpu.VMEM((GROUP * rows, HD), bf),
+            pltpu.VMEM((HD, cols), jnp.float32),
+            pltpu.VMEM((cols, HD), jnp.float32),
         ],
     )
     aliases = {4 + slots + len(term) + i: i for i in range(len(earlier))}
@@ -187,7 +227,7 @@
     total = jnp.sum(parts_ref[...].astype(jnp.float32), axis=0)
     own_ref[...] = total[:, :shard]
     extras = total[0, shard:]
-    term_ref[...] = extras[0:2] + extras[2:4] + extras[4:6]
+    term_ref[...] = (extras[0:KVH] + extras[KVH : 2 * KVH] + extras[2 * KVH : 3 * KVH])[:, :HD]
 
 
 def relay(parts, held):
@@ -199,7 +239,7 @@
         out_specs=[vmem, vmem, whole],
         out_shape=[
             jax.ShapeDtypeStruct((count, padded - EXTRA, width), jnp.float32),
-            jax.ShapeDtypeStruct((2, width), jnp.float32),
+            jax.ShapeDtypeStruct((KVH, HD), jnp.float32),
             jax.ShapeDtypeStruct(held.shape, held.dtype),
         ],
         input_output_aliases={1: 2},
@@ -242,15 +282,6 @@
 def exchange_sum(term, axis, step):
     size = lax.axis_size(axis)
     return term + lax.ppermute(term, axis, [(i, i ^ step) for i in range(size)])
-
-
-def three_parts(value):
-    parts = []
-    for _ in range(3):
-        high = lax.reduce_precision(value, 8, 7)
-        parts.append(high.astype(jnp.bfloat16))
-        value = value - high
-    return jnp.stack(parts)
 
 
 def shards(resp_q, resp_kv, prompt_kv, bias, prompt_len, resp_len, d_out):
@@ -264,9 +295,9 @@
     term = jnp.sum(live_sum.reshape(KVH, GROUP, HD), axis=1)
     pieces = gather_pieces(own, sizes)
     term = exchange_sum(term, "prompt", HEAD_STEPS[0])
-    arrived = pieces[4][0, :1, :HD].astype(jnp.float32) + pieces[5][0, :1, :HD].astype(jnp.float32)
-    term = exchange_sum(term + 0.0 * arrived, "prompt", HEAD_STEPS[1])
-    term = jnp.pad(three_parts(term).reshape(6, 2 * HD), ((0, EXTRA - 6), (0, 0)))
+    term = term + 0.0 * pieces[6][0, :1, :HD].astype(jnp.float32)
+    for step in HEAD_STEPS[1:]:
+        term = exchange_sum(term, "prompt", step)
     resp_side = by_head(resp_kv[0, 0], bias)
     me = lax.axis_index("resp")
     y, x = me // sizes[1], me % sizes[1]

time: 89.5 us -> 83 us (0.927); the launches traced: 89.2 us -> 81.7 us
  waiting for transfers between devices: 13.2 us -> 8.38 us
  Pallas kernels: 30.7 us -> 27.1 us
  starting transfers between devices: 35.3 us -> 36.3 us
    ppermute x7, waiting for transfers between devices: 9.82 us -> 4.12 us  [move(): lax.ppermute(value, 'resp', [(y * nx + x, (y + dy) % ny * nx + (x + dx) %...]
    pallas_call x2, Pallas kernels: 29.9 us -> 26.3 us  [attend(): pl.pallas_call(functools.partial(attend_body, slots, rows, shard, len(ter...]
    unnamed x29 -> x28, local copies, waits for them, and re-layouts: 2.33 us -> 1.75 us
  transfers between devices with their start and end apart: 14 -> 14, of which waited for: 6 -> 6; matrix products, arithmetic and copies ran while one was open for 4% -> 5% of each run, Pallas kernels for 17% -> 16%
where the time goes in v3:
time: 83 us; the launch traced here: 81.7 us
  starting transfers between devices  36.3 us (44%)
  Pallas kernels  27.1 us (33%)
  waiting for transfers between devices  8.38 us (10%)
  local copies, waits for them, and re-layouts  6.01 us (7%)
  between operations  2.21 us (3%)
  other arithmetic  1.66 us (2%)
    pallas_call x2, Pallas kernels, attend(): pl.pallas_call(functools.partial(attend_body, slots, rows, shard, len(ter...  26.3 us
    ppermute x5, starting transfers between devices, exchange_sum(): return term + lax.ppermute(term, axis, [(i, i ^ step) for i in range(size)])  15.6 us
    ppermute x7, starting transfers between devices, move(): lax.ppermute(value, 'resp', [(y * nx + x, (y + dy) % ny * nx + (x + dx) %...  8.38 us
    all_to_all x1, starting transfers between devices, shards(): parts = lax.all_to_all(parts, 'resp', 0, 0)  7.1 us
    all_to_all x1, starting transfers between devices, shards(): arrived = lax.all_to_all(held, 'resp', 0, 0)  5.23 us
    ppermute x7, waiting for transfers between devices, move(): lax.ppermute(value, 'resp', [(y * nx + x, (y + dy) % ny * nx + (x + dx) %...  4.12 us
    ppermute x5, waiting for transfers between devices, exchange_sum(): return term + lax.ppermute(term, axis, [(i, i ^ step) for i in range(size)])  3.65 us
    unnamed x28, local copies, waits for them, and re-layouts  1.75 us
  transfers between devices with their start and end apart: 14, of which 6 were waited for; matrix products, arithmetic and copies ran while one was open for 5% of the time, Pallas kernels for 16%

profile of v3, /device:TPU:2, one launch (start us, length us, event | category | flops | bytes accessed | tf_op | source)
XLA Modules:
  0.0 81.7 jit_solution(18183523903921474809)
XLA Ops:
  0.6 0.8 stack.41
  1.5 1.1 %copy.30 = bf16[1,128,2,512]{1,3,2,0:T(8,128)(2,1)S(1)} copy(bf16[1,128,2,512]{3,2,1,0:T(2,128)(2,1)} %param.9) | data formatting | bytes 524288 | tf_op args[2]
  2.8 2.3 %collective-permute-start.2 = (bf16[4,128,256]{2,1,0:T(8,128)(2,1)S(1)}, bf16[4,128,256]{2,1,0:T(8,128)(2,1)S(1)}, u32[]{:S(2)}, u32[]{:S(2)}) collective-permute-start(bf16[4,128,256]{2,1,0:T(8,128)(2,1)S(1)} %copy_bitcast_fusion.1.refs_0_), channel_id=1, source_target_pairs={{0,96},{32,0},{64,32},{96,64},{128,224},{160,128},{192,160},{224,1... | collective-permute-start | bytes 786440 | tf_op jit(solution)/shard_map/ppermute | solution.py:264
  5.2 1.3 %collective-permute-start = (bf16[4,128,256]{2,1,0:T(8,128)(2,1)S(1)}, bf16[4,128,256]{2,1,0:T(8,128)(2,1)S(1)}, u32[]{:S(2)}, u32[]{:S(2)}) collective-permute-start(bf16[4,128,256]{2,1,0:T(8,128)(2,1)S(1)} %copy_bitcast_fusion.1.refs_0_), channel_id=1, source_target_pairs={{0,128},{32,160},{64,192},{96,224},{128,0},{160,32},{192,64},{224,... | collective-permute-start | bytes 786440 | tf_op jit(solution)/shard_map/ppermute | solution.py:264
  7.2 0.3 select_reduce_fusion
  7.6 3.0 %collective-permute-start.7 = (f32[4,128]{1,0:T(4,128)S(1)}, f32[4,128]{1,0:T(4,128)S(1)}, u32[]{:S(2)}, u32[]{:S(2)}) collective-permute-start(f32[4,128]{1,0:T(4,128)S(1)} %reduce_sum.28), channel_id=1, source_target_pairs={{0,16},{1,17},{2,18},{3,19},{4,20},{5,21},{6,22},{7,23},{8,24},{9,... | collective-permute-start | bytes 6152 | tf_op jit(solution)/shard_map/ppermute | solution.py:284
  10.5 0.5 copy.27
  11.1 0.2 copy.28
  11.3 1.3 %collective-permute-start.5 = (bf16[4,128,256]{2,1,0:T(8,128)(2,1)S(1)}, bf16[4,128,256]{2,1,0:T(8,128)(2,1)S(1)}, u32[]{:S(2)}, u32[]{:S(2)}) collective-permute-start(bf16[4,128,256]{2,1,0:T(8,128)(2,1)S(1)} %collective-permute-done.2.refs_3_), channel_id=1, source_target_pairs={{0,96},{32,0},{64,32},{96,64},{128,224},{160,128},{192,160},{224,1... | collective-permute-start | bytes 786440 | tf_op jit(solution)/shard_map/ppermute | solution.py:264
  12.8 0.8 collective-permute-start.4
  13.5 1.2 %collective-permute-start.3 = (bf16[4,128,256]{2,1,0:T(8,128)(2,1)S(1)}, bf16[4,128,256]{2,1,0:T(8,128)(2,1)S(1)}, u32[]{:S(2)}, u32[]{:S(2)}) collective-permute-start(bf16[4,128,256]{2,1,0:T(8,128)(2,1)S(1)} %collective-permute-done.refs_1_), channel_id=1, source_target_pairs={{0,32},{32,64},{64,96},{96,0},{128,160},{160,192},{192,224},{224,1... | collective-permute-start | bytes 786440 | tf_op jit(solution)/shard_map/ppermute | solution.py:264
  14.8 3.6 %collective-permute-done.5.refs_6_ = bf16[4,128,256]{2,1,0:T(8,128)(2,1)S(1)} collective-permute-done((bf16[4,128,256]{2,1,0:T(8,128)(2,1)S(1)}, bf16[4,128,256]{2,1,0:T(8,128)(2,1)S(1)}, u32[]{:S(2)}, u32[]{:S(2)}) %collective-permute-start.5) | collective-permute-done | bytes 262176 | tf_op jit(solution)/shard_map/ppermute | solution.py:264
  18.3 1.4 %collective-permute-start.6 = (bf16[4,128,256]{2,1,0:T(8,128)(2,1)S(1)}, bf16[4,128,256]{2,1,0:T(8,128)(2,1)S(1)}, u32[]{:S(2)}, u32[]{:S(2)}) collective-permute-start(bf16[4,128,256]{2,1,0:T(8,128)(2,1)S(1)} %collective-permute-done.5.refs_6_), channel_id=1, source_target_pairs={{0,128},{32,160},{64,192},{96,224},{128,0},{160,32},{192,64},{224,... | collective-permute-start | bytes 786440 | tf_op jit(solution)/shard_map/ppermute | solution.py:264
  19.7 3.5 %collective-permute-start.8 = (f32[4,128]{1,0:T(4,128)S(1)}, f32[4,128]{1,0:T(4,128)S(1)}, u32[]{:S(2)}, u32[]{:S(2)}) collective-permute-start(f32[4,128]{1,0:T(4,128)S(1)} %add_add_fusion), channel_id=1, source_target_pairs={{0,4},{1,5},{2,6},{3,7},{4,0},{5,1},{6,2},{7,3},{8,12},{9,13},{10,... | collective-permute-start | bytes 6152 | tf_op jit(solution)/shard_map/ppermute | solution.py:284
  24.0 0.8 %collective-permute-done.8 = f32[4,128]{1,0:T(4,128)S(1)} collective-permute-done((f32[4,128]{1,0:T(4,128)S(1)}, f32[4,128]{1,0:T(4,128)S(1)}, u32[]{:S(2)}, u32[]{:S(2)}) %collective-permute-start.8) | collective-permute-done | bytes 2080 | tf_op jit(solution)/shard_map/ppermute | solution.py:284
  24.9 0.5 collective-permute-done.6.refs_7_
  25.4 13.0 %attend.2 = (bf16[256,2560]{1,0:T(8,128)(2,1)}, bf16[256,2560]{1,0:T(8,128)(2,1)}, bf16[2,256,256]{2,1,0:T(8,128)(2,1)S(1)}, bf16[8,2,144,256]{3,2,1,0:T(8,128)(2,1)}) custom-call(s32[10]{0:T(128)S(1)} %concatenate.15.meta, bf16[256,2560]{1,0:T(8,128)(2,1)} %bitcast.47, bf16[256,2560]{1,0:T(8,128)(2,1)} %bitcast.43, ...), custom_call_target="tpu_custom_call" | custom-call | flops 5033164800 | bytes 2621440 | tf_op jit(solution)/shard_map/attend/pallas_call | solution.py:204
  38.5 7.1 %all-to-all-start = ((bf16[8,2,144,256]{3,2,1,0:T(8,128)(2,1)}), bf16[8,2,144,256]{3,2,1,0:T(8,128)(2,1)S(1)}, u32[]{:S(2)}, u32[]{:S(2)}) async-start(bf16[8,2,144,256]{3,2,1,0:T(8,128)(2,1)} %get-tuple-element.22), calls=%async_computation | async-start | bytes 2359296 | tf_op jit(solution)/shard_map/all_to_all | solution.py:308
  45.6 13.2 %attend.3 = (bf16[256,2560]{1,0:T(8,128)(2,1)}, bf16[256,2560]{1,0:T(8,128)(2,1)}, bf16[2,256,256]{2,1,0:T(8,128)(2,1)S(1)}, bf16[8,2,128,256]{3,2,1,0:T(8,128)(2,1)}) custom-call(s32[10]{0:T(128)S(1)} %concatenate.15.meta, bf16[256,2560]{1,0:T(8,128)(2,1)} %bitcast.48, bf16[256,2560]{1,0:T(8,128)(2,1)} %bitcast.44, ...), custom_call_target="tpu_custom_call", output_to_operand_aliasing={{0}: (12, {}), {1}: (13, {})} | custom-call | flops 5033164800 | bytes 2621440 | tf_op jit(solution)/shard_map/attend/pallas_call | solution.py:204
  58.9 0.6 all-to-all-done.parts_ref
  59.5 0.8 %relay.1 = (f32[2,128,256]{2,1,0:T(8,128)}, f32[4,128]{1,0:T(4,128)}, bf16[8,2,128,256]{3,2,1,0:T(8,128)(2,1)}) custom-call(bf16[8,2,144,256]{3,2,1,0:T(8,128)(2,1)S(1)} %all-to-all-done.parts_ref, bf16[8,2,128,256]{3,2,1,0:T(8,128)(2,1)} %get-tuple-element.23.held_ref), custom_call_target="tpu_custom_call", output_to_operand_aliasing={{2}: (1, {})} | custom-call | tf_op jit(solution)/shard_map/relay/pallas_call | solution.py:236
  60.3 5.2 %all-to-all-start.1 = ((bf16[8,2,128,256]{3,2,1,0:T(8,128)(2,1)}), bf16[8,2,128,256]{3,2,1,0:T(8,128)(2,1)S(1)}, u32[]{:S(2)}, u32[]{:S(2)}) async-start(bf16[8,2,128,256]{3,2,1,0:T(8,128)(2,1)} %get-tuple-element.25), calls=%async_computation.1 | async-start | bytes 2097152 | tf_op jit(solution)/shard_map/all_to_all | solution.py:311
  65.5 1.2 %collective-permute-done.9 = f32[4,128]{1,0:T(4,128)S(1)} collective-permute-done((f32[4,128]{1,0:T(4,128)S(1)}, f32[4,128]{1,0:T(4,128)S(1)}, u32[]{:S(2)}, u32[]{:S(2)}) %collective-permute-start.9) | collective-permute-done | bytes 2080 | tf_op jit(solution)/shard_map/ppermute | solution.py:284
  66.7 1.9 %collective-permute-start.10 = (f32[4,128]{1,0:T(4,128)S(1)}, f32[4,128]{1,0:T(4,128)S(1)}, u32[]{:S(2)}, u32[]{:S(2)}) collective-permute-start(f32[4,128]{1,0:T(4,128)S(1)} %add.148), channel_id=1, source_target_pairs={{0,2},{1,3},{2,0},{3,1},{4,6},{5,7},{6,4},{7,5},{8,10},{9,11},{10,... | collective-permute-start | bytes 6152 | tf_op jit(solution)/shard_map/ppermute | solution.py:284
  68.6 1.7 %collective-permute-done.10 = f32[4,128]{1,0:T(4,128)S(1)} collective-permute-done((f32[4,128]{1,0:T(4,128)S(1)}, f32[4,128]{1,0:T(4,128)S(1)}, u32[]{:S(2)}, u32[]{:S(2)}) %collective-permute-start.10) | collective-permute-done | bytes 2080 | tf_op jit(solution)/shard_map/ppermute | solution.py:284
  70.3 7.2 %collective-permute-start.11 = (f32[4,128]{1,0:T(4,128)S(1)}, f32[4,128]{1,0:T(4,128)S(1)}, u32[]{:S(2)}, u32[]{:S(2)}) collective-permute-start(f32[4,128]{1,0:T(4,128)S(1)} %add.149), channel_id=1, source_target_pairs={{0,8},{1,9},{2,10},{3,11},{4,12},{5,13},{6,14},{7,15},{8,0},{9,1},... | collective-permute-start | bytes 6152 | tf_op jit(solution)/shard_map/ppermute | solution.py:284
  77.7 0.7 copy.33
  78.4 1.0 %broadcast_in_dim_reshape.6 = bf16[1,1,256,2,512]{4,3,2,1,0:T(2,128)(2,1)} reshape(bf16[256,2,4,128]{3,2,1,0:T(4,128)(2,1)S(1)} %copy.33) | data formatting | bytes 1048576 | tf_op jit(solution)/shard_map/broadcast_in_dim;reshape | solution.py:320
  79.4 0.6 multiply_bitcast_fusion
  80.2 0.3 maximum_bitcast_fusion
  80.5 0.3 copy.34
  80.9 0.8 broadcast_in_dim_reshape.7
  (55 shorter events, 0.9 us)
Async XLA Ops:
  0.6 6.5 %copy-start.9 = (bf16[1,1,256,2560]{3,2,1,0:T(8,128)(2,1)S(1)}, bf16[1,1,256,2560]{3,2,1,0:T(8,128)(2,1)}, u32[]{:S(2)}) copy-start(bf16[1,1,256,2560]{3,2,1,0:T(8,128)(2,1)} %param.13) | copy-start | bytes 3932164
  2.8 7.8 %copy-start.10 = (bf16[1,1,256,2,512]{4,3,2,1,0:T(2,128)(2,1)S(1)}, bf16[1,1,256,2,512]{4,3,2,1,0:T(2,128)(2,1)}, u32[]{:S(2)}) copy-start(bf16[1,1,256,2,512]{4,3,2,1,0:T(2,128)(2,1)} %param.8) | copy-start | bytes 1572868
  2.8 22.6 %copy-start.1 = (bf16[4,128,256]{2,1,0:T(8,128)(2,1)}, bf16[4,128,256]{2,1,0:T(8,128)(2,1)S(1)}, u32[]{:S(2)}) copy-start(bf16[4,128,256]{2,1,0:T(8,128)(2,1)S(1)} %copy_bitcast_fusion.1.refs_0_) | copy-start | bytes 786436
  2.8 8.5 %collective-permute-start.2 = (bf16[4,128,256]{2,1,0:T(8,128)(2,1)S(1)}, bf16[4,128,256]{2,1,0:T(8,128)(2,1)S(1)}, u32[]{:S(2)}, u32[]{:S(2)}) collective-permute-start(bf16[4,128,256]{2,1,0:T(8,128)(2,1)S(1)} %copy_bitcast_fusion.1.refs_0_), channel_id=1, source_target_pairs={{0,96},{32,0},{64,32},{96,64},{128,224},{160,128},{192,160},{224,1... | collective-permute-start | bytes 786440 | tf_op jit(solution)/shard_map/ppermute | solution.py:264
  5.2 19.7 %collective-permute-start.1 = (bf16[4,128,256]{2,1,0:T(8,128)(2,1)S(1)}, bf16[4,128,256]{2,1,0:T(8,128)(2,1)S(1)}, u32[]{:S(2)}, u32[]{:S(2)}) collective-permute-start(bf16[4,128,256]{2,1,0:T(8,128)(2,1)S(1)} %copy_bitcast_fusion.1.refs_0_), channel_id=1, source_target_pairs={{0,32},{32,64},{64,96},{96,0},{128,160},{160,192},{192,224},{224,1... | collective-permute-start | bytes 786440 | tf_op jit(solution)/shard_map/ppermute | solution.py:264
  5.2 8.4 %collective-permute-start = (bf16[4,128,256]{2,1,0:T(8,128)(2,1)S(1)}, bf16[4,128,256]{2,1,0:T(8,128)(2,1)S(1)}, u32[]{:S(2)}, u32[]{:S(2)}) collective-permute-start(bf16[4,128,256]{2,1,0:T(8,128)(2,1)S(1)} %copy_bitcast_fusion.1.refs_0_), channel_id=1, source_target_pairs={{0,128},{32,160},{64,192},{96,224},{128,0},{160,32},{192,64},{224,... | collective-permute-start | bytes 786440 | tf_op jit(solution)/shard_map/ppermute | solution.py:264
  7.6 12.2 %collective-permute-start.7 = (f32[4,128]{1,0:T(4,128)S(1)}, f32[4,128]{1,0:T(4,128)S(1)}, u32[]{:S(2)}, u32[]{:S(2)}) collective-permute-start(f32[4,128]{1,0:T(4,128)S(1)} %reduce_sum.28), channel_id=1, source_target_pairs={{0,16},{1,17},{2,18},{3,19},{4,20},{5,21},{6,22},{7,23},{8,24},{9,... | collective-permute-start | bytes 6152 | tf_op jit(solution)/shard_map/ppermute | solution.py:284
  11.3 27.1 %copy-start.2 = (bf16[4,128,256]{2,1,0:T(8,128)(2,1)}, bf16[4,128,256]{2,1,0:T(8,128)(2,1)S(1)}, u32[]{:S(2)}) copy-start(bf16[4,128,256]{2,1,0:T(8,128)(2,1)S(1)} %collective-permute-done.2.refs_3_) | copy-start | bytes 786436
  11.3 7.0 %collective-permute-start.5 = (bf16[4,128,256]{2,1,0:T(8,128)(2,1)S(1)}, bf16[4,128,256]{2,1,0:T(8,128)(2,1)S(1)}, u32[]{:S(2)}, u32[]{:S(2)}) collective-permute-start(bf16[4,128,256]{2,1,0:T(8,128)(2,1)S(1)} %collective-permute-done.2.refs_3_), channel_id=1, source_target_pairs={{0,96},{32,0},{64,32},{96,64},{128,224},{160,128},{192,160},{224,1... | collective-permute-start | bytes 786440 | tf_op jit(solution)/shard_map/ppermute | solution.py:264
  12.8 25.7 %copy-start = (bf16[4,256,256]{2,1,0:T(8,128)(2,1)}, bf16[4,256,256]{2,1,0:T(8,128)(2,1)S(1)}, u32[]{:S(2)}) copy-start(bf16[4,256,256]{2,1,0:T(8,128)(2,1)S(1)} %copy_bitcast_fusion.kvr_ref) | copy-start | bytes 1572868
  12.8 12.1 %collective-permute-start.4 = (bf16[4,128,256]{2,1,0:T(8,128)(2,1)S(1)}, bf16[4,128,256]{2,1,0:T(8,128)(2,1)S(1)}, u32[]{:S(2)}, u32[]{:S(2)}) collective-permute-start(bf16[4,128,256]{2,1,0:T(8,128)(2,1)S(1)} %collective-permute-done.2.refs_3_), channel_id=1, source_target_pairs={{0,128},{32,160},{64,192},{96,224},{128,0},{160,32},{192,64},{224,... | collective-permute-start | bytes 786440 | tf_op jit(solution)/shard_map/ppermute | solution.py:264
  13.5 24.9 %copy-start.4 = (bf16[4,128,256]{2,1,0:T(8,128)(2,1)}, bf16[4,128,256]{2,1,0:T(8,128)(2,1)S(1)}, u32[]{:S(2)}) copy-start(bf16[4,128,256]{2,1,0:T(8,128)(2,1)S(1)} %collective-permute-done.refs_1_) | copy-start | bytes 786436
  13.5 11.3 %collective-permute-start.3 = (bf16[4,128,256]{2,1,0:T(8,128)(2,1)S(1)}, bf16[4,128,256]{2,1,0:T(8,128)(2,1)S(1)}, u32[]{:S(2)}, u32[]{:S(2)}) collective-permute-start(bf16[4,128,256]{2,1,0:T(8,128)(2,1)S(1)} %collective-permute-done.refs_1_), channel_id=1, source_target_pairs={{0,32},{32,64},{64,96},{96,0},{128,160},{160,192},{192,224},{224,1... | collective-permute-start | bytes 786440 | tf_op jit(solution)/shard_map/ppermute | solution.py:264
  18.3 20.1 %copy-start.5 = (bf16[4,128,256]{2,1,0:T(8,128)(2,1)}, bf16[4,128,256]{2,1,0:T(8,128)(2,1)S(1)}, u32[]{:S(2)}) copy-start(bf16[4,128,256]{2,1,0:T(8,128)(2,1)S(1)} %collective-permute-done.5.refs_6_) | copy-start | bytes 786436
  18.3 7.1 %collective-permute-start.6 = (bf16[4,128,256]{2,1,0:T(8,128)(2,1)S(1)}, bf16[4,128,256]{2,1,0:T(8,128)(2,1)S(1)}, u32[]{:S(2)}, u32[]{:S(2)}) collective-permute-start(bf16[4,128,256]{2,1,0:T(8,128)(2,1)S(1)} %collective-permute-done.5.refs_6_), channel_id=1, source_target_pairs={{0,128},{32,160},{64,192},{96,224},{128,0},{160,32},{192,64},{224,... | collective-permute-start | bytes 786440 | tf_op jit(solution)/shard_map/ppermute | solution.py:264
  19.7 5.1 %collective-permute-start.8 = (f32[4,128]{1,0:T(4,128)S(1)}, f32[4,128]{1,0:T(4,128)S(1)}, u32[]{:S(2)}, u32[]{:S(2)}) collective-permute-start(f32[4,128]{1,0:T(4,128)S(1)} %add_add_fusion), channel_id=1, source_target_pairs={{0,4},{1,5},{2,6},{3,7},{4,0},{5,1},{6,2},{7,3},{8,12},{9,13},{10,... | collective-permute-start | bytes 6152 | tf_op jit(solution)/shard_map/ppermute | solution.py:284
  24.8 13.7 %copy-start.3 = (bf16[4,128,256]{2,1,0:T(8,128)(2,1)}, bf16[4,128,256]{2,1,0:T(8,128)(2,1)S(1)}, u32[]{:S(2)}) copy-start(bf16[4,128,256]{2,1,0:T(8,128)(2,1)S(1)} %collective-permute-done.1.refs_2_) | copy-start | bytes 786436
  24.8 13.7 %copy-start.6 = (bf16[4,128,256]{2,1,0:T(8,128)(2,1)}, bf16[4,128,256]{2,1,0:T(8,128)(2,1)S(1)}, u32[]{:S(2)}) copy-start(bf16[4,128,256]{2,1,0:T(8,128)(2,1)S(1)} %collective-permute-done.4.refs_5_) | copy-start | bytes 786436
  24.9 13.6 %copy-start.7 = (bf16[4,128,256]{2,1,0:T(8,128)(2,1)}, bf16[4,128,256]{2,1,0:T(8,128)(2,1)S(1)}, u32[]{:S(2)}) copy-start(bf16[4,128,256]{2,1,0:T(8,128)(2,1)S(1)} %collective-permute-done.3.refs_4_) | copy-start | bytes 786436
  25.4 13.1 %copy-start.8 = (bf16[4,128,256]{2,1,0:T(8,128)(2,1)}, bf16[4,128,256]{2,1,0:T(8,128)(2,1)S(1)}, u32[]{:S(2)}) copy-start(bf16[4,128,256]{2,1,0:T(8,128)(2,1)S(1)} %collective-permute-done.6.refs_7_) | copy-start | bytes 786436
  38.5 20.9 %all-to-all-start = ((bf16[8,2,144,256]{3,2,1,0:T(8,128)(2,1)}), bf16[8,2,144,256]{3,2,1,0:T(8,128)(2,1)S(1)}, u32[]{:S(2)}, u32[]{:S(2)}) async-start(bf16[8,2,144,256]{3,2,1,0:T(8,128)(2,1)} %get-tuple-element.22), calls=%async_computation | async-start | bytes 2359296 | tf_op jit(solution)/shard_map/all_to_all | solution.py:308
  60.3 5.2 %copy-start.12 = (f32[4,128]{1,0:T(4,128)S(1)}, f32[4,128]{1,0:T(4,128)}, u32[]{:S(2)}) copy-start(f32[4,128]{1,0:T(4,128)} %get-tuple-element.26) | copy-start | bytes 6148
  60.3 19.7 %all-to-all-start.1 = ((bf16[8,2,128,256]{3,2,1,0:T(8,128)(2,1)}), bf16[8,2,128,256]{3,2,1,0:T(8,128)(2,1)S(1)}, u32[]{:S(2)}, u32[]{:S(2)}) async-start(bf16[8,2,128,256]{3,2,1,0:T(8,128)(2,1)} %get-tuple-element.25), calls=%async_computation.1 | async-start | bytes 2097152 | tf_op jit(solution)/shard_map/all_to_all | solution.py:311
  65.5 1.2 %collective-permute-start.9 = (f32[4,128]{1,0:T(4,128)S(1)}, f32[4,128]{1,0:T(4,128)S(1)}, u32[]{:S(2)}, u32[]{:S(2)}) collective-permute-start(f32[4,128]{1,0:T(4,128)S(1)} %copy-done.12), channel_id=1, source_target_pairs={{0,1},{1,0},{2,3},{3,2},{4,5},{5,4},{6,7},{7,6},{8,9},{9,8},{10,11... | collective-permute-start | bytes 6152 | tf_op jit(solution)/shard_map/ppermute | solution.py:284
  66.7 3.6 %collective-permute-start.10 = (f32[4,128]{1,0:T(4,128)S(1)}, f32[4,128]{1,0:T(4,128)S(1)}, u32[]{:S(2)}, u32[]{:S(2)}) collective-permute-start(f32[4,128]{1,0:T(4,128)S(1)} %add.148), channel_id=1, source_target_pairs={{0,2},{1,3},{2,0},{3,1},{4,6},{5,7},{6,4},{7,5},{8,10},{9,11},{10,... | collective-permute-start | bytes 6152 | tf_op jit(solution)/shard_map/ppermute | solution.py:284
  70.3 9.1 %collective-permute-start.11 = (f32[4,128]{1,0:T(4,128)S(1)}, f32[4,128]{1,0:T(4,128)S(1)}, u32[]{:S(2)}, u32[]{:S(2)}) collective-permute-start(f32[4,128]{1,0:T(4,128)S(1)} %add.149), channel_id=1, source_target_pairs={{0,8},{1,9},{2,10},{3,11},{4,12},{5,13},{6,14},{7,15},{8,0},{9,1},... | collective-permute-start | bytes 6152 | tf_op jit(solution)/shard_map/ppermute | solution.py:284
  77.7 1.7 %copy-start.11 = (f32[2,128,256]{2,1,0:T(8,128)S(1)}, f32[2,128,256]{2,1,0:T(8,128)}, u32[]{:S(2)}) copy-start(f32[2,128,256]{2,1,0:T(8,128)} %get-tuple-element.24) | copy-start | bytes 786436

commit v4 on v3

--- a/solution.py
+++ b/solution.py
@@ -140,7 +140,9 @@
                     stage(t - lag, b)
     dk = (dk_scr[...] * SCALE).T
     dv = dv_scr[...]
+    own_rows = pl.ds(pl.multiple_of(pl.program_id(0) * shard, shard), shard)
     if term:
+        extra_rows = slice(parts_ref.shape[1] - EXTRA, parts_ref.shape[1])
         rest, split = term_ref[...], []
         for _ in range(3):
             split.append(rest.astype(jnp.bfloat16).astype(jnp.float32))
@@ -149,12 +151,12 @@
         extras = jnp.concatenate(split, axis=0).astype(jnp.bfloat16)
     for s in range(slots):
         at = slice(s * shard, (s + 1) * shard)
-        out = parts_ref.at[meta[2 + s], 0]
+        out = parts_ref.at[meta[2 + s]]
+        out[own_rows, :HD] = jnp.where(seen[s], dk[at], 0.0).astype(jnp.bfloat16)
+        out[own_rows, HD:] = jnp.where(seen[s], dv[at], 0.0).astype(jnp.bfloat16)
         if term:
-            out[shard:, :HD] = extras
-            out[shard:, HD:] = jnp.zeros_like(extras)
-        out[:shard, :HD] = jnp.where(seen[s], dk[at], 0.0).astype(jnp.bfloat16)
-        out[:shard, HD:] = jnp.where(seen[s], dv[at], 0.0).astype(jnp.bfloat16)
+            out[extra_rows, :HD] = extras
+            out[extra_rows, HD:] = jnp.zeros_like(extras)
     dkvr_ref[0, :, :HD] = dk[prompt:].astype(jnp.bfloat16)
     dkvr_ref[0, :, HD:] = dv[prompt:].astype(jnp.bfloat16)
 
@@ -172,7 +174,7 @@
     whole = pl.BlockSpec(memory_space=pl.ANY)
     head = pl.BlockSpec((rows, wide), lambda g, m: (0, first + g))
     piece = pl.BlockSpec((1, shard, 2 * HD), lambda g, m: (first + g, 0, 0))
-    part = (slots, count, shard + EXTRA * len(term), 2 * HD)
+    part = (slots, count * shard + EXTRA * len(term), 2 * HD)
     grid_spec = pltpu.PrefetchScalarGridSpec(
         num_scalar_prefetch=1,
         grid=(count,),
@@ -184,7 +186,7 @@
             head,
             head,
             pl.BlockSpec((1, rows, 2 * HD), lambda g, m: (g, 0, 0)),
-            pl.BlockSpec((slots, 1, *part[2:]), lambda g, m: (0, g, 0, 0)),
+            pl.BlockSpec(part, lambda g, m: (0, 0, 0)),
         ],
         scratch_shapes=[
             pltpu.VMEM((cols, HD), bf),
@@ -223,22 +225,22 @@
 
 
 def relay_body(parts_ref, held_ref, own_ref, term_ref, held_out):
-    shard = own_ref.shape[1]
+    rows = own_ref.shape[0]
     total = jnp.sum(parts_ref[...].astype(jnp.float32), axis=0)
-    own_ref[...] = total[:, :shard]
-    extras = total[0, shard:]
-    term_ref[...] = (extras[0:KVH] + extras[KVH : 2 * KVH] + extras[2 * KVH : 3 * KVH])[:, :HD]
+    own_ref[...] = total[:rows]
+    extras = total[rows:, :HD]
+    term_ref[...] = extras[0:KVH] + extras[KVH : 2 * KVH] + extras[2 * KVH : 3 * KVH]
 
 
 def relay(parts, held):
     vmem, whole = pl.BlockSpec(memory_space=pltpu.VMEM), pl.BlockSpec(memory_space=pl.ANY)
-    _, count, padded, width = parts.shape
+    _, padded, width = parts.shape
     return pl.pallas_call(
         relay_body,
         in_specs=[vmem, whole],
         out_specs=[vmem, vmem, whole],
         out_shape=[
-            jax.ShapeDtypeStruct((count, padded - EXTRA, width), jnp.float32),
+            jax.ShapeDtypeStruct((padded - EXTRA, width), jnp.float32),
             jax.ShapeDtypeStruct((KVH, HD), jnp.float32),
             jax.ShapeDtypeStruct(held.shape, held.dtype),
         ],
@@ -249,9 +251,9 @@
 
 def by_head(pairs, bias):
     rows = pairs.shape[0]
-    biased = pairs.astype(jnp.float32) + jnp.stack([jnp.zeros_like(bias), bias])
-    split = biased.astype(jnp.bfloat16).reshape(rows, 2, KVH, HD)
-    return split.transpose(2, 0, 1, 3).reshape(KVH, rows, 2 * HD)
+    keys = pairs[:, 0].reshape(rows, KVH, HD)
+    values = (pairs[:, 1].astype(jnp.float32) + bias).astype(jnp.bfloat16).reshape(rows, KVH, HD)
+    return jnp.concatenate([keys, values], axis=2).transpose(1, 0, 2)
 
 
 def by_pair(heads):
@@ -313,7 +315,7 @@
         term = exchange_sum(term, "prompt", step)
     d_bias = term.reshape(KVH * HD) / (members * prompts)
     last_grad = jnp.sum(arrived.astype(jnp.float32), axis=0)
-    prompt_grad = jnp.concatenate([first_grad, last_grad]).astype(jnp.bfloat16)
+    prompt_grad = jnp.concatenate([first_grad, last_grad]).astype(jnp.bfloat16).reshape(own.shape)
     return (
         attn_out[None, None],
         d_q[None, None],

time: 83 us -> 81.8 us (0.986)
    unnamed x28 -> x30, local copies, waits for them, and re-layouts: 1.75 us -> 1.85 us
  transfers between devices with their start and end apart: 14 -> 14, of which waited for: 6 -> 5; matrix products, arithmetic and copies ran while one was open for 5% -> 5% of each run, Pallas kernels for 16% -> 16%
where the time goes in v4:
time: 81.8 us; the launch traced here: 81.1 us
  starting transfers between devices  36.5 us (45%)
  Pallas kernels  27.3 us (33%)
  waiting for transfers between devices  8.11 us (10%)
  local copies, waits for them, and re-layouts  5.56 us (7%)
  between operations  2.29 us (3%)
  other arithmetic  1.37 us (2%)
    pallas_call x2, Pallas kernels, attend(): pl.pallas_call(functools.partial(attend_body, slots, rows, shard, len(ter...  26.5 us
    ppermute x5, starting transfers between devices, exchange_sum(): return term + lax.ppermute(term, axis, [(i, i ^ step) for i in range(size)])  15.6 us
    ppermute x7, starting transfers between devices, move(): lax.ppermute(value, 'resp', [(y * nx + x, (y + dy) % ny * nx + (x + dx) %...  8.06 us
    all_to_all x1, starting transfers between devices, shards(): parts = lax.all_to_all(parts, 'resp', 0, 0)  6.92 us
    all_to_all x1, starting transfers between devices, shards(): arrived = lax.all_to_all(held, 'resp', 0, 0)  5.82 us
    ppermute x7, waiting for transfers between devices, move(): lax.ppermute(value, 'resp', [(y * nx + x, (y + dy) % ny * nx + (x + dx) %...  4.43 us
    ppermute x5, waiting for transfers between devices, exchange_sum(): return term + lax.ppermute(term, axis, [(i, i ^ step) for i in range(size)])  3.65 us
    unnamed x30, local copies, waits for them, and re-layouts  1.85 us
  transfers between devices with their start and end apart: 14, of which 5 were waited for; matrix products, arithmetic and copies ran while one was open for 5% of the time, Pallas kernels for 16%

profile of v4, /device:TPU:2, one launch (start us, length us, event | category | flops | bytes accessed | tf_op | source)
XLA Modules:
  0.0 81.1 jit_solution(6151701819519582278)
XLA Ops:
  0.7 1.3 %copy.20 = bf16[1,128,2,512]{1,3,2,0:T(8,128)(2,1)S(1)} copy(bf16[1,128,2,512]{3,2,1,0:T(2,128)(2,1)} %param.9) | data formatting | bytes 524288 | tf_op args[2]
  1.9 0.1 copy.22
  2.3 2.3 %collective-permute-start.2 = (bf16[4,128,256]{2,1,0:T(8,128)(2,1)S(1)}, bf16[4,128,256]{2,1,0:T(8,128)(2,1)S(1)}, u32[]{:S(2)}, u32[]{:S(2)}) collective-permute-start(bf16[4,128,256]{2,1,0:T(8,128)(2,1)S(1)} %maximum_bitcast_fusion.1.refs_0_), channel_id=1, source_target_pairs={{0,96},{32,0},{64,32},{96,64},{128,224},{160,128},{192,160},{224,1... | collective-permute-start | bytes 786440 | tf_op jit(solution)/shard_map/ppermute | solution.py:266
  4.7 1.3 %collective-permute-start = (bf16[4,128,256]{2,1,0:T(8,128)(2,1)S(1)}, bf16[4,128,256]{2,1,0:T(8,128)(2,1)S(1)}, u32[]{:S(2)}, u32[]{:S(2)}) collective-permute-start(bf16[4,128,256]{2,1,0:T(8,128)(2,1)S(1)} %maximum_bitcast_fusion.1.refs_0_), channel_id=1, source_target_pairs={{0,128},{32,160},{64,192},{96,224},{128,0},{160,32},{192,64},{224,... | collective-permute-start | bytes 786440 | tf_op jit(solution)/shard_map/ppermute | solution.py:266
  6.7 0.3 select_reduce_fusion
  7.0 3.0 %collective-permute-start.7 = (f32[4,128]{1,0:T(4,128)S(1)}, f32[4,128]{1,0:T(4,128)S(1)}, u32[]{:S(2)}, u32[]{:S(2)}) collective-permute-start(f32[4,128]{1,0:T(4,128)S(1)} %reduce_sum.28), channel_id=1, source_target_pairs={{0,16},{1,17},{2,18},{3,19},{4,20},{5,21},{6,22},{7,23},{8,24},{9,... | collective-permute-start | bytes 6152 | tf_op jit(solution)/shard_map/ppermute | solution.py:286
  10.0 0.5 copy.17
  10.6 0.2 copy.19
  10.8 0.1 copy.18
  11.0 1.3 %collective-permute-start.5 = (bf16[4,128,256]{2,1,0:T(8,128)(2,1)S(1)}, bf16[4,128,256]{2,1,0:T(8,128)(2,1)S(1)}, u32[]{:S(2)}, u32[]{:S(2)}) collective-permute-start(bf16[4,128,256]{2,1,0:T(8,128)(2,1)S(1)} %collective-permute-done.2.refs_3_), channel_id=1, source_target_pairs={{0,96},{32,0},{64,32},{96,64},{128,224},{160,128},{192,160},{224,1... | collective-permute-start | bytes 786440 | tf_op jit(solution)/shard_map/ppermute | solution.py:266
  12.4 0.6 collective-permute-start.4
  13.0 1.2 %collective-permute-start.3 = (bf16[4,128,256]{2,1,0:T(8,128)(2,1)S(1)}, bf16[4,128,256]{2,1,0:T(8,128)(2,1)S(1)}, u32[]{:S(2)}, u32[]{:S(2)}) collective-permute-start(bf16[4,128,256]{2,1,0:T(8,128)(2,1)S(1)} %collective-permute-done.refs_1_), channel_id=1, source_target_pairs={{0,32},{32,64},{64,96},{96,0},{128,160},{160,192},{192,224},{224,1... | collective-permute-start | bytes 786440 | tf_op jit(solution)/shard_map/ppermute | solution.py:266
  14.3 3.7 %collective-permute-done.5.refs_6_ = bf16[4,128,256]{2,1,0:T(8,128)(2,1)S(1)} collective-permute-done((bf16[4,128,256]{2,1,0:T(8,128)(2,1)S(1)}, bf16[4,128,256]{2,1,0:T(8,128)(2,1)S(1)}, u32[]{:S(2)}, u32[]{:S(2)}) %collective-permute-start.5) | collective-permute-done | bytes 262176 | tf_op jit(solution)/shard_map/ppermute | solution.py:266
  18.0 1.2 %collective-permute-start.6 = (bf16[4,128,256]{2,1,0:T(8,128)(2,1)S(1)}, bf16[4,128,256]{2,1,0:T(8,128)(2,1)S(1)}, u32[]{:S(2)}, u32[]{:S(2)}) collective-permute-start(bf16[4,128,256]{2,1,0:T(8,128)(2,1)S(1)} %collective-permute-done.5.refs_6_), channel_id=1, source_target_pairs={{0,128},{32,160},{64,192},{96,224},{128,0},{160,32},{192,64},{224,... | collective-permute-start | bytes 786440 | tf_op jit(solution)/shard_map/ppermute | solution.py:266
  19.2 3.5 %collective-permute-start.8 = (f32[4,128]{1,0:T(4,128)S(1)}, f32[4,128]{1,0:T(4,128)S(1)}, u32[]{:S(2)}, u32[]{:S(2)}) collective-permute-start(f32[4,128]{1,0:T(4,128)S(1)} %add_add_fusion), channel_id=1, source_target_pairs={{0,4},{1,5},{2,6},{3,7},{4,0},{5,1},{6,2},{7,3},{8,12},{9,13},{10,... | collective-permute-start | bytes 6152 | tf_op jit(solution)/shard_map/ppermute | solution.py:286
  23.5 0.8 %collective-permute-done.8 = f32[4,128]{1,0:T(4,128)S(1)} collective-permute-done((f32[4,128]{1,0:T(4,128)S(1)}, f32[4,128]{1,0:T(4,128)S(1)}, u32[]{:S(2)}, u32[]{:S(2)}) %collective-permute-start.8) | collective-permute-done | bytes 2080 | tf_op jit(solution)/shard_map/ppermute | solution.py:286
  24.4 0.7 collective-permute-done.6.refs_7_
  25.1 13.2 %attend.2 = (bf16[256,2560]{1,0:T(8,128)(2,1)}, bf16[256,2560]{1,0:T(8,128)(2,1)}, bf16[2,256,256]{2,1,0:T(8,128)(2,1)S(1)}, bf16[8,272,256]{2,1,0:T(8,128)(2,1)}) custom-call(s32[10]{0:T(128)S(1)} %concatenate.16.meta, bf16[256,2560]{1,0:T(8,128)(2,1)} %bitcast.48, bf16[256,2560]{1,0:T(8,128)(2,1)} %bitcast.38, ...), custom_call_target="tpu_custom_call" | custom-call | flops 5033164800 | bytes 2621440 | tf_op jit(solution)/shard_map/attend/pallas_call | solution.py:206
  38.3 6.9 %all-to-all-start = ((bf16[8,272,256]{2,1,0:T(8,128)(2,1)}), bf16[8,272,256]{2,1,0:T(8,128)(2,1)S(1)}, u32[]{:S(2)}, u32[]{:S(2)}) async-start(bf16[8,272,256]{2,1,0:T(8,128)(2,1)} %get-tuple-element.22), calls=%async_computation | async-start | bytes 2228224 | tf_op jit(solution)/shard_map/all_to_all | solution.py:310
  45.3 13.3 %attend.3 = (bf16[256,2560]{1,0:T(8,128)(2,1)}, bf16[256,2560]{1,0:T(8,128)(2,1)}, bf16[2,256,256]{2,1,0:T(8,128)(2,1)S(1)}, bf16[8,256,256]{2,1,0:T(8,128)(2,1)}) custom-call(s32[10]{0:T(128)S(1)} %concatenate.16.meta, bf16[256,2560]{1,0:T(8,128)(2,1)} %bitcast.49, bf16[256,2560]{1,0:T(8,128)(2,1)} %bitcast.39, ...), custom_call_target="tpu_custom_call", output_to_operand_aliasing={{0}: (12, {}), {1}: (13, {})} | custom-call | flops 5033164800 | bytes 2621440 | tf_op jit(solution)/shard_map/attend/pallas_call | solution.py:206
  58.6 0.8 %relay.1 = (f32[256,256]{1,0:T(8,128)}, f32[4,128]{1,0:T(4,128)}, bf16[8,256,256]{2,1,0:T(8,128)(2,1)}) custom-call(bf16[8,272,256]{2,1,0:T(8,128)(2,1)S(1)} %all-to-all-done.parts_ref, bf16[8,256,256]{2,1,0:T(8,128)(2,1)} %get-tuple-element.23.held_ref), custom_call_target="tpu_custom_call", output_to_operand_aliasing={{2}: (1, {})} | custom-call | tf_op jit(solution)/shard_map/relay/pallas_call | solution.py:238
  59.4 5.8 %all-to-all-start.1 = ((bf16[8,256,256]{2,1,0:T(8,128)(2,1)}), bf16[8,256,256]{2,1,0:T(8,128)(2,1)S(1)}, u32[]{:S(2)}, u32[]{:S(2)}) async-start(bf16[8,256,256]{2,1,0:T(8,128)(2,1)} %get-tuple-element.25), calls=%async_computation.1 | async-start | bytes 2097152 | tf_op jit(solution)/shard_map/all_to_all | solution.py:313
  65.2 1.2 %collective-permute-done.9 = f32[4,128]{1,0:T(4,128)S(1)} collective-permute-done((f32[4,128]{1,0:T(4,128)S(1)}, f32[4,128]{1,0:T(4,128)S(1)}, u32[]{:S(2)}, u32[]{:S(2)}) %collective-permute-start.9) | collective-permute-done | bytes 2080 | tf_op jit(solution)/shard_map/ppermute | solution.py:286
  66.4 1.9 %collective-permute-start.10 = (f32[4,128]{1,0:T(4,128)S(1)}, f32[4,128]{1,0:T(4,128)S(1)}, u32[]{:S(2)}, u32[]{:S(2)}) collective-permute-start(f32[4,128]{1,0:T(4,128)S(1)} %add.146), channel_id=1, source_target_pairs={{0,2},{1,3},{2,0},{3,1},{4,6},{5,7},{6,4},{7,5},{8,10},{9,11},{10,... | collective-permute-start | bytes 6152 | tf_op jit(solution)/shard_map/ppermute | solution.py:286
  68.3 1.7 %collective-permute-done.10 = f32[4,128]{1,0:T(4,128)S(1)} collective-permute-done((f32[4,128]{1,0:T(4,128)S(1)}, f32[4,128]{1,0:T(4,128)S(1)}, u32[]{:S(2)}, u32[]{:S(2)}) %collective-permute-start.10) | collective-permute-done | bytes 2080 | tf_op jit(solution)/shard_map/ppermute | solution.py:286
  70.0 7.2 %collective-permute-start.11 = (f32[4,128]{1,0:T(4,128)S(1)}, f32[4,128]{1,0:T(4,128)S(1)}, u32[]{:S(2)}, u32[]{:S(2)}) collective-permute-start(f32[4,128]{1,0:T(4,128)S(1)} %add.147), channel_id=1, source_target_pairs={{0,8},{1,9},{2,10},{3,11},{4,12},{5,13},{6,14},{7,15},{8,0},{9,1},... | collective-permute-start | bytes 6152 | tf_op jit(solution)/shard_map/ppermute | solution.py:286
  77.4 0.7 copy.23
  78.1 1.0 %broadcast_in_dim_reshape.6 = bf16[1,1,256,2,512]{4,3,2,1,0:T(2,128)(2,1)} reshape(bf16[256,2,4,128]{3,2,1,0:T(4,128)(2,1)S(1)} %copy.23) | data formatting | bytes 1048576 | tf_op jit(solution)/shard_map/broadcast_in_dim;reshape | solution.py:322
  79.1 0.6 multiply_bitcast_fusion
  79.7 0.1 reduce
  79.9 0.3 copy.24
  80.3 0.8 broadcast_in_dim_reshape.7
  (60 shorter events, 0.9 us)
Async XLA Ops:
  0.6 1.6 %copy-start.12 = (f32[512]{0:T(512)S(1)}, f32[512]{0:T(512)}, u32[]{:S(2)}) copy-start(f32[512]{0:T(512)} %param.10) | copy-start | bytes 6148
  0.6 6.0 %copy-start.9 = (bf16[1,1,256,2560]{3,2,1,0:T(8,128)(2,1)S(1)}, bf16[1,1,256,2560]{3,2,1,0:T(8,128)(2,1)}, u32[]{:S(2)}) copy-start(bf16[1,1,256,2560]{3,2,1,0:T(8,128)(2,1)} %param.13) | copy-start | bytes 3932164
  2.2 7.8 %copy-start.10 = (bf16[1,1,256,2,512]{4,3,2,1,0:T(2,128)(2,1)S(1)}, bf16[1,1,256,2,512]{4,3,2,1,0:T(2,128)(2,1)}, u32[]{:S(2)}) copy-start(bf16[1,1,256,2,512]{4,3,2,1,0:T(2,128)(2,1)} %param.8) | copy-start | bytes 1572868
  2.3 22.8 %copy-start.1 = (bf16[4,128,256]{2,1,0:T(8,128)(2,1)}, bf16[4,128,256]{2,1,0:T(8,128)(2,1)S(1)}, u32[]{:S(2)}) copy-start(bf16[4,128,256]{2,1,0:T(8,128)(2,1)S(1)} %maximum_bitcast_fusion.1.refs_0_) | copy-start | bytes 786436
  2.3 8.6 %collective-permute-start.2 = (bf16[4,128,256]{2,1,0:T(8,128)(2,1)S(1)}, bf16[4,128,256]{2,1,0:T(8,128)(2,1)S(1)}, u32[]{:S(2)}, u32[]{:S(2)}) collective-permute-start(bf16[4,128,256]{2,1,0:T(8,128)(2,1)S(1)} %maximum_bitcast_fusion.1.refs_0_), channel_id=1, source_target_pairs={{0,96},{32,0},{64,32},{96,64},{128,224},{160,128},{192,160},{224,1... | collective-permute-start | bytes 786440 | tf_op jit(solution)/shard_map/ppermute | solution.py:266
  4.7 19.7 %collective-permute-start.1 = (bf16[4,128,256]{2,1,0:T(8,128)(2,1)S(1)}, bf16[4,128,256]{2,1,0:T(8,128)(2,1)S(1)}, u32[]{:S(2)}, u32[]{:S(2)}) collective-permute-start(bf16[4,128,256]{2,1,0:T(8,128)(2,1)S(1)} %maximum_bitcast_fusion.1.refs_0_), channel_id=1, source_target_pairs={{0,32},{32,64},{64,96},{96,0},{128,160},{160,192},{192,224},{224,1... | collective-permute-start | bytes 786440 | tf_op jit(solution)/shard_map/ppermute | solution.py:266
  4.7 8.4 %collective-permute-start = (bf16[4,128,256]{2,1,0:T(8,128)(2,1)S(1)}, bf16[4,128,256]{2,1,0:T(8,128)(2,1)S(1)}, u32[]{:S(2)}, u32[]{:S(2)}) collective-permute-start(bf16[4,128,256]{2,1,0:T(8,128)(2,1)S(1)} %maximum_bitcast_fusion.1.refs_0_), channel_id=1, source_target_pairs={{0,128},{32,160},{64,192},{96,224},{128,0},{160,32},{192,64},{224,... | collective-permute-start | bytes 786440 | tf_op jit(solution)/shard_map/ppermute | solution.py:266
  7.0 12.2 %collective-permute-start.7 = (f32[4,128]{1,0:T(4,128)S(1)}, f32[4,128]{1,0:T(4,128)S(1)}, u32[]{:S(2)}, u32[]{:S(2)}) collective-permute-start(f32[4,128]{1,0:T(4,128)S(1)} %reduce_sum.28), channel_id=1, source_target_pairs={{0,16},{1,17},{2,18},{3,19},{4,20},{5,21},{6,22},{7,23},{8,24},{9,... | collective-permute-start | bytes 6152 | tf_op jit(solution)/shard_map/ppermute | solution.py:286
  10.9 27.3 %copy-start.2 = (bf16[4,128,256]{2,1,0:T(8,128)(2,1)}, bf16[4,128,256]{2,1,0:T(8,128)(2,1)S(1)}, u32[]{:S(2)}) copy-start(bf16[4,128,256]{2,1,0:T(8,128)(2,1)S(1)} %collective-permute-done.2.refs_3_) | copy-start | bytes 786436
  11.0 7.0 %collective-permute-start.5 = (bf16[4,128,256]{2,1,0:T(8,128)(2,1)S(1)}, bf16[4,128,256]{2,1,0:T(8,128)(2,1)S(1)}, u32[]{:S(2)}, u32[]{:S(2)}) collective-permute-start(bf16[4,128,256]{2,1,0:T(8,128)(2,1)S(1)} %collective-permute-done.2.refs_3_), channel_id=1, source_target_pairs={{0,96},{32,0},{64,32},{96,64},{128,224},{160,128},{192,160},{224,1... | collective-permute-start | bytes 786440 | tf_op jit(solution)/shard_map/ppermute | solution.py:266
  12.4 25.9 %copy-start = (bf16[4,256,256]{2,1,0:T(8,128)(2,1)}, bf16[4,256,256]{2,1,0:T(8,128)(2,1)S(1)}, u32[]{:S(2)}) copy-start(bf16[4,256,256]{2,1,0:T(8,128)(2,1)S(1)} %maximum_bitcast_fusion.kvr_ref) | copy-start | bytes 1572868
  12.4 11.9 %collective-permute-start.4 = (bf16[4,128,256]{2,1,0:T(8,128)(2,1)S(1)}, bf16[4,128,256]{2,1,0:T(8,128)(2,1)S(1)}, u32[]{:S(2)}, u32[]{:S(2)}) collective-permute-start(bf16[4,128,256]{2,1,0:T(8,128)(2,1)S(1)} %collective-permute-done.2.refs_3_), channel_id=1, source_target_pairs={{0,128},{32,160},{64,192},{96,224},{128,0},{160,32},{192,64},{224,... | collective-permute-start | bytes 786440 | tf_op jit(solution)/shard_map/ppermute | solution.py:266
  13.0 25.2 %copy-start.4 = (bf16[4,128,256]{2,1,0:T(8,128)(2,1)}, bf16[4,128,256]{2,1,0:T(8,128)(2,1)S(1)}, u32[]{:S(2)}) copy-start(bf16[4,128,256]{2,1,0:T(8,128)(2,1)S(1)} %collective-permute-done.refs_1_) | copy-start | bytes 786436
  13.0 11.3 %collective-permute-start.3 = (bf16[4,128,256]{2,1,0:T(8,128)(2,1)S(1)}, bf16[4,128,256]{2,1,0:T(8,128)(2,1)S(1)}, u32[]{:S(2)}, u32[]{:S(2)}) collective-permute-start(bf16[4,128,256]{2,1,0:T(8,128)(2,1)S(1)} %collective-permute-done.refs_1_), channel_id=1, source_target_pairs={{0,32},{32,64},{64,96},{96,0},{128,160},{160,192},{192,224},{224,1... | collective-permute-start | bytes 786440 | tf_op jit(solution)/shard_map/ppermute | solution.py:266
  18.0 20.3 %copy-start.5 = (bf16[4,128,256]{2,1,0:T(8,128)(2,1)}, bf16[4,128,256]{2,1,0:T(8,128)(2,1)S(1)}, u32[]{:S(2)}) copy-start(bf16[4,128,256]{2,1,0:T(8,128)(2,1)S(1)} %collective-permute-done.5.refs_6_) | copy-start | bytes 786436
  18.0 7.1 %collective-permute-start.6 = (bf16[4,128,256]{2,1,0:T(8,128)(2,1)S(1)}, bf16[4,128,256]{2,1,0:T(8,128)(2,1)S(1)}, u32[]{:S(2)}, u32[]{:S(2)}) collective-permute-start(bf16[4,128,256]{2,1,0:T(8,128)(2,1)S(1)} %collective-permute-done.5.refs_6_), channel_id=1, source_target_pairs={{0,128},{32,160},{64,192},{96,224},{128,0},{160,32},{192,64},{224,... | collective-permute-start | bytes 786440 | tf_op jit(solution)/shard_map/ppermute | solution.py:266
  19.2 5.1 %collective-permute-start.8 = (f32[4,128]{1,0:T(4,128)S(1)}, f32[4,128]{1,0:T(4,128)S(1)}, u32[]{:S(2)}, u32[]{:S(2)}) collective-permute-start(f32[4,128]{1,0:T(4,128)S(1)} %add_add_fusion), channel_id=1, source_target_pairs={{0,4},{1,5},{2,6},{3,7},{4,0},{5,1},{6,2},{7,3},{8,12},{9,13},{10,... | collective-permute-start | bytes 6152 | tf_op jit(solution)/shard_map/ppermute | solution.py:286
  24.3 14.0 %copy-start.3 = (bf16[4,128,256]{2,1,0:T(8,128)(2,1)}, bf16[4,128,256]{2,1,0:T(8,128)(2,1)S(1)}, u32[]{:S(2)}) copy-start(bf16[4,128,256]{2,1,0:T(8,128)(2,1)S(1)} %collective-permute-done.1.refs_2_) | copy-start | bytes 786436
  24.3 14.0 %copy-start.6 = (bf16[4,128,256]{2,1,0:T(8,128)(2,1)}, bf16[4,128,256]{2,1,0:T(8,128)(2,1)S(1)}, u32[]{:S(2)}) copy-start(bf16[4,128,256]{2,1,0:T(8,128)(2,1)S(1)} %collective-permute-done.4.refs_5_) | copy-start | bytes 786436
  24.3 14.0 %copy-start.7 = (bf16[4,128,256]{2,1,0:T(8,128)(2,1)}, bf16[4,128,256]{2,1,0:T(8,128)(2,1)S(1)}, u32[]{:S(2)}) copy-start(bf16[4,128,256]{2,1,0:T(8,128)(2,1)S(1)} %collective-permute-done.3.refs_4_) | copy-start | bytes 786436
  25.1 13.3 %copy-start.8 = (bf16[4,128,256]{2,1,0:T(8,128)(2,1)}, bf16[4,128,256]{2,1,0:T(8,128)(2,1)S(1)}, u32[]{:S(2)}) copy-start(bf16[4,128,256]{2,1,0:T(8,128)(2,1)S(1)} %collective-permute-done.6.refs_7_) | copy-start | bytes 786436
  38.3 20.2 %all-to-all-start = ((bf16[8,272,256]{2,1,0:T(8,128)(2,1)}), bf16[8,272,256]{2,1,0:T(8,128)(2,1)S(1)}, u32[]{:S(2)}, u32[]{:S(2)}) async-start(bf16[8,272,256]{2,1,0:T(8,128)(2,1)} %get-tuple-element.22), calls=%async_computation | async-start | bytes 2228224 | tf_op jit(solution)/shard_map/all_to_all | solution.py:310
  59.4 5.8 %copy-start.13 = (f32[4,128]{1,0:T(4,128)S(1)}, f32[4,128]{1,0:T(4,128)}, u32[]{:S(2)}) copy-start(f32[4,128]{1,0:T(4,128)} %get-tuple-element.26) | copy-start | bytes 6148
  59.4 20.3 %all-to-all-start.1 = ((bf16[8,256,256]{2,1,0:T(8,128)(2,1)}), bf16[8,256,256]{2,1,0:T(8,128)(2,1)S(1)}, u32[]{:S(2)}, u32[]{:S(2)}) async-start(bf16[8,256,256]{2,1,0:T(8,128)(2,1)} %get-tuple-element.25), calls=%async_computation.1 | async-start | bytes 2097152 | tf_op jit(solution)/shard_map/all_to_all | solution.py:313
  65.2 1.2 %collective-permute-start.9 = (f32[4,128]{1,0:T(4,128)S(1)}, f32[4,128]{1,0:T(4,128)S(1)}, u32[]{:S(2)}, u32[]{:S(2)}) collective-permute-start(f32[4,128]{1,0:T(4,128)S(1)} %copy-done.13), channel_id=1, source_target_pairs={{0,1},{1,0},{2,3},{3,2},{4,5},{5,4},{6,7},{7,6},{8,9},{9,8},{10,11... | collective-permute-start | bytes 6152 | tf_op jit(solution)/shard_map/ppermute | solution.py:286
  66.4 3.6 %collective-permute-start.10 = (f32[4,128]{1,0:T(4,128)S(1)}, f32[4,128]{1,0:T(4,128)S(1)}, u32[]{:S(2)}, u32[]{:S(2)}) collective-permute-start(f32[4,128]{1,0:T(4,128)S(1)} %add.146), channel_id=1, source_target_pairs={{0,2},{1,3},{2,0},{3,1},{4,6},{5,7},{6,4},{7,5},{8,10},{9,11},{10,... | collective-permute-start | bytes 6152 | tf_op jit(solution)/shard_map/ppermute | solution.py:286
  70.0 9.1 %collective-permute-start.11 = (f32[4,128]{1,0:T(4,128)S(1)}, f32[4,128]{1,0:T(4,128)S(1)}, u32[]{:S(2)}, u32[]{:S(2)}) collective-permute-start(f32[4,128]{1,0:T(4,128)S(1)} %add.147), channel_id=1, source_target_pairs={{0,8},{1,9},{2,10},{3,11},{4,12},{5,13},{6,14},{7,15},{8,0},{9,1},... | collective-permute-start | bytes 6152 | tf_op jit(solution)/shard_map/ppermute | solution.py:286
  77.4 1.7 %copy-start.11 = (f32[256,256]{1,0:T(8,128)S(1)}, f32[256,256]{1,0:T(8,128)}, u32[]{:S(2)}) copy-start(f32[256,256]{1,0:T(8,128)} %get-tuple-element.24) | copy-start | bytes 786436

commit v5 on v4

--- a/solution.py
+++ b/solution.py
@@ -275,7 +275,7 @@
     left, right = move(own, 0, 1, sizes), move(own, 0, -1, sizes)
     beside_left, beside_right = move(beside, 0, 1, sizes), move(right, 1, 0, sizes)
     opposite = move(right, 0, -1, sizes)
-    beside_opposite = move(opposite, 1, 0, sizes)
+    beside_opposite = move(beside_right, 0, -1, sizes)
     return [own, beside, left, right, beside_left, beside_right, opposite, beside_opposite]
 
 
@@ -297,7 +297,7 @@
     term = jnp.sum(live_sum.reshape(KVH, GROUP, HD), axis=1)
     pieces = gather_pieces(own, sizes)
     term = exchange_sum(term, "prompt", HEAD_STEPS[0])
-    term = term + 0.0 * pieces[6][0, :1, :HD].astype(jnp.float32)
+    term = term + 0.0 * pieces[1][0, :1, :HD].astype(jnp.float32)
     for step in HEAD_STEPS[1:]:
         term = exchange_sum(term, "prompt", step)
     resp_side = by_head(resp_kv[0, 0], bias)

time: 81.8 us -> 81.4 us (level)
  transfers between devices with their start and end apart: 14 -> 14, of which waited for: 5 -> 4; matrix products, arithmetic and copies ran while one was open for 5% -> 5% of each run, Pallas kernels for 16% -> 16%
where the time goes in v5:
time: 81.4 us; the launch traced here: 81.1 us
  starting transfers between devices  37.1 us (46%)
  Pallas kernels  27.3 us (34%)
  waiting for transfers between devices  7.43 us (9%)
  local copies, waits for them, and re-layouts  5.56 us (7%)
  between operations  2.29 us (3%)
  other arithmetic  1.37 us (2%)
    pallas_call x2, Pallas kernels, attend(): pl.pallas_call(functools.partial(attend_body, slots, rows, shard, len(ter...  26.5 us
    ppermute x5, starting transfers between devices, exchange_sum(): return term + lax.ppermute(term, axis, [(i, i ^ step) for i in range(size)])  15.6 us
    ppermute x7, starting transfers between devices, move(): lax.ppermute(value, 'resp', [(y * nx + x, (y + dy) % ny * nx + (x + dx) %...  8.38 us
    all_to_all x1, starting transfers between devices, shards(): parts = lax.all_to_all(parts, 'resp', 0, 0)  7.28 us
    all_to_all x1, starting transfers between devices, shards(): arrived = lax.all_to_all(held, 'resp', 0, 0)  5.84 us
    ppermute x7, waiting for transfers between devices, move(): lax.ppermute(value, 'resp', [(y * nx + x, (y + dy) % ny * nx + (x + dx) %...  3.77 us
    ppermute x5, waiting for transfers between devices, exchange_sum(): return term + lax.ppermute(term, axis, [(i, i ^ step) for i in range(size)])  3.65 us
    unnamed x30, local copies, waits for them, and re-layouts  1.85 us
  transfers between devices with their start and end apart: 14, of which 4 were waited for; matrix products, arithmetic and copies ran while one was open for 5% of the time, Pallas kernels for 16%

profile of v5, /device:TPU:2, one launch (start us, length us, event | category | flops | bytes accessed | tf_op | source)
XLA Modules:
  0.0 81.1 jit_solution(15183101041113502276)
XLA Ops:
  0.7 1.3 %copy.20 = bf16[1,128,2,512]{1,3,2,0:T(8,128)(2,1)S(1)} copy(bf16[1,128,2,512]{3,2,1,0:T(2,128)(2,1)} %param.9) | data formatting | bytes 524288 | tf_op args[2]
  1.9 0.1 copy.22
  2.3 2.3 %collective-permute-start.2 = (bf16[4,128,256]{2,1,0:T(8,128)(2,1)S(1)}, bf16[4,128,256]{2,1,0:T(8,128)(2,1)S(1)}, u32[]{:S(2)}, u32[]{:S(2)}) collective-permute-start(bf16[4,128,256]{2,1,0:T(8,128)(2,1)S(1)} %maximum_bitcast_fusion.1.refs_0_), channel_id=1, source_target_pairs={{0,96},{32,0},{64,32},{96,64},{128,224},{160,128},{192,160},{224,1... | collective-permute-start | bytes 786440 | tf_op jit(solution)/shard_map/ppermute | solution.py:266
  4.7 1.3 %collective-permute-start = (bf16[4,128,256]{2,1,0:T(8,128)(2,1)S(1)}, bf16[4,128,256]{2,1,0:T(8,128)(2,1)S(1)}, u32[]{:S(2)}, u32[]{:S(2)}) collective-permute-start(bf16[4,128,256]{2,1,0:T(8,128)(2,1)S(1)} %maximum_bitcast_fusion.1.refs_0_), channel_id=1, source_target_pairs={{0,128},{32,160},{64,192},{96,224},{128,0},{160,32},{192,64},{224,... | collective-permute-start | bytes 786440 | tf_op jit(solution)/shard_map/ppermute | solution.py:266
  6.7 0.3 select_reduce_fusion
  7.0 3.0 %collective-permute-start.7 = (f32[4,128]{1,0:T(4,128)S(1)}, f32[4,128]{1,0:T(4,128)S(1)}, u32[]{:S(2)}, u32[]{:S(2)}) collective-permute-start(f32[4,128]{1,0:T(4,128)S(1)} %reduce_sum.28), channel_id=1, source_target_pairs={{0,16},{1,17},{2,18},{3,19},{4,20},{5,21},{6,22},{7,23},{8,24},{9,... | collective-permute-start | bytes 6152 | tf_op jit(solution)/shard_map/ppermute | solution.py:286
  10.0 0.5 copy.17
  10.6 0.2 copy.19
  10.8 0.1 copy.18
  11.0 1.1 %collective-permute-start.4 = (bf16[4,128,256]{2,1,0:T(8,128)(2,1)S(1)}, bf16[4,128,256]{2,1,0:T(8,128)(2,1)S(1)}, u32[]{:S(2)}, u32[]{:S(2)}) collective-permute-start(bf16[4,128,256]{2,1,0:T(8,128)(2,1)S(1)} %collective-permute-done.2.refs_3_), channel_id=1, source_target_pairs={{0,128},{32,160},{64,192},{96,224},{128,0},{160,32},{192,64},{224,... | collective-permute-start | bytes 786440 | tf_op jit(solution)/shard_map/ppermute | solution.py:266
  12.1 0.9 %collective-permute-start.5 = (bf16[4,128,256]{2,1,0:T(8,128)(2,1)S(1)}, bf16[4,128,256]{2,1,0:T(8,128)(2,1)S(1)}, u32[]{:S(2)}, u32[]{:S(2)}) collective-permute-start(bf16[4,128,256]{2,1,0:T(8,128)(2,1)S(1)} %collective-permute-done.2.refs_3_), channel_id=1, source_target_pairs={{0,96},{32,0},{64,32},{96,64},{128,224},{160,128},{192,160},{224,1... | collective-permute-start | bytes 786440 | tf_op jit(solution)/shard_map/ppermute | solution.py:266
  13.0 1.2 %collective-permute-start.3 = (bf16[4,128,256]{2,1,0:T(8,128)(2,1)S(1)}, bf16[4,128,256]{2,1,0:T(8,128)(2,1)S(1)}, u32[]{:S(2)}, u32[]{:S(2)}) collective-permute-start(bf16[4,128,256]{2,1,0:T(8,128)(2,1)S(1)} %collective-permute-done.refs_1_), channel_id=1, source_target_pairs={{0,32},{32,64},{64,96},{96,0},{128,160},{160,192},{192,224},{224,1... | collective-permute-start | bytes 786440 | tf_op jit(solution)/shard_map/ppermute | solution.py:266
  14.3 3.7 %collective-permute-done.4.refs_5_ = bf16[4,128,256]{2,1,0:T(8,128)(2,1)S(1)} collective-permute-done((bf16[4,128,256]{2,1,0:T(8,128)(2,1)S(1)}, bf16[4,128,256]{2,1,0:T(8,128)(2,1)S(1)}, u32[]{:S(2)}, u32[]{:S(2)}) %collective-permute-start.4) | collective-permute-done | bytes 262176 | tf_op jit(solution)/shard_map/ppermute | solution.py:266
  18.0 1.6 %collective-permute-start.6 = (bf16[4,128,256]{2,1,0:T(8,128)(2,1)S(1)}, bf16[4,128,256]{2,1,0:T(8,128)(2,1)S(1)}, u32[]{:S(2)}, u32[]{:S(2)}) collective-permute-start(bf16[4,128,256]{2,1,0:T(8,128)(2,1)S(1)} %collective-permute-done.4.refs_5_), channel_id=1, source_target_pairs={{0,96},{32,0},{64,32},{96,64},{128,224},{160,128},{192,160},{224,1... | collective-permute-start | bytes 786440 | tf_op jit(solution)/shard_map/ppermute | solution.py:266
  19.5 3.5 %collective-permute-start.8 = (f32[4,128]{1,0:T(4,128)S(1)}, f32[4,128]{1,0:T(4,128)S(1)}, u32[]{:S(2)}, u32[]{:S(2)}) collective-permute-start(f32[4,128]{1,0:T(4,128)S(1)} %add_add_fusion), channel_id=1, source_target_pairs={{0,4},{1,5},{2,6},{3,7},{4,0},{5,1},{6,2},{7,3},{8,12},{9,13},{10,... | collective-permute-start | bytes 6152 | tf_op jit(solution)/shard_map/ppermute | solution.py:286
  23.8 0.8 %collective-permute-done.8 = f32[4,128]{1,0:T(4,128)S(1)} collective-permute-done((f32[4,128]{1,0:T(4,128)S(1)}, f32[4,128]{1,0:T(4,128)S(1)}, u32[]{:S(2)}, u32[]{:S(2)}) %collective-permute-start.8) | collective-permute-done | bytes 2080 | tf_op jit(solution)/shard_map/ppermute | solution.py:286
  24.7 13.2 %attend.2 = (bf16[256,2560]{1,0:T(8,128)(2,1)}, bf16[256,2560]{1,0:T(8,128)(2,1)}, bf16[2,256,256]{2,1,0:T(8,128)(2,1)S(1)}, bf16[8,272,256]{2,1,0:T(8,128)(2,1)}) custom-call(s32[10]{0:T(128)S(1)} %concatenate.16.meta, bf16[256,2560]{1,0:T(8,128)(2,1)} %bitcast.48, bf16[256,2560]{1,0:T(8,128)(2,1)} %bitcast.38, ...), custom_call_target="tpu_custom_call" | custom-call | flops 5033164800 | bytes 2621440 | tf_op jit(solution)/shard_map/attend/pallas_call | solution.py:206
  38.0 7.3 %all-to-all-start = ((bf16[8,272,256]{2,1,0:T(8,128)(2,1)}), bf16[8,272,256]{2,1,0:T(8,128)(2,1)S(1)}, u32[]{:S(2)}, u32[]{:S(2)}) async-start(bf16[8,272,256]{2,1,0:T(8,128)(2,1)} %get-tuple-element.22), calls=%async_computation | async-start | bytes 2228224 | tf_op jit(solution)/shard_map/all_to_all | solution.py:310
  45.3 13.3 %attend.3 = (bf16[256,2560]{1,0:T(8,128)(2,1)}, bf16[256,2560]{1,0:T(8,128)(2,1)}, bf16[2,256,256]{2,1,0:T(8,128)(2,1)S(1)}, bf16[8,256,256]{2,1,0:T(8,128)(2,1)}) custom-call(s32[10]{0:T(128)S(1)} %concatenate.16.meta, bf16[256,2560]{1,0:T(8,128)(2,1)} %bitcast.49, bf16[256,2560]{1,0:T(8,128)(2,1)} %bitcast.39, ...), custom_call_target="tpu_custom_call", output_to_operand_aliasing={{0}: (12, {}), {1}: (13, {})} | custom-call | flops 5033164800 | bytes 2621440 | tf_op jit(solution)/shard_map/attend/pallas_call | solution.py:206
  58.6 0.8 %relay.1 = (f32[256,256]{1,0:T(8,128)}, f32[4,128]{1,0:T(4,128)}, bf16[8,256,256]{2,1,0:T(8,128)(2,1)}) custom-call(bf16[8,272,256]{2,1,0:T(8,128)(2,1)S(1)} %all-to-all-done.parts_ref, bf16[8,256,256]{2,1,0:T(8,128)(2,1)} %get-tuple-element.23.held_ref), custom_call_target="tpu_custom_call", output_to_operand_aliasing={{2}: (1, {})} | custom-call | tf_op jit(solution)/shard_map/relay/pallas_call | solution.py:238
  59.4 5.8 %all-to-all-start.1 = ((bf16[8,256,256]{2,1,0:T(8,128)(2,1)}), bf16[8,256,256]{2,1,0:T(8,128)(2,1)S(1)}, u32[]{:S(2)}, u32[]{:S(2)}) async-start(bf16[8,256,256]{2,1,0:T(8,128)(2,1)} %get-tuple-element.25), calls=%async_computation.1 | async-start | bytes 2097152 | tf_op jit(solution)/shard_map/all_to_all | solution.py:313
  65.3 1.2 %collective-permute-done.9 = f32[4,128]{1,0:T(4,128)S(1)} collective-permute-done((f32[4,128]{1,0:T(4,128)S(1)}, f32[4,128]{1,0:T(4,128)S(1)}, u32[]{:S(2)}, u32[]{:S(2)}) %collective-permute-start.9) | collective-permute-done | bytes 2080 | tf_op jit(solution)/shard_map/ppermute | solution.py:286
  66.4 1.9 %collective-permute-start.10 = (f32[4,128]{1,0:T(4,128)S(1)}, f32[4,128]{1,0:T(4,128)S(1)}, u32[]{:S(2)}, u32[]{:S(2)}) collective-permute-start(f32[4,128]{1,0:T(4,128)S(1)} %add.146), channel_id=1, source_target_pairs={{0,2},{1,3},{2,0},{3,1},{4,6},{5,7},{6,4},{7,5},{8,10},{9,11},{10,... | collective-permute-start | bytes 6152 | tf_op jit(solution)/shard_map/ppermute | solution.py:286
  68.3 1.7 %collective-permute-done.10 = f32[4,128]{1,0:T(4,128)S(1)} collective-permute-done((f32[4,128]{1,0:T(4,128)S(1)}, f32[4,128]{1,0:T(4,128)S(1)}, u32[]{:S(2)}, u32[]{:S(2)}) %collective-permute-start.10) | collective-permute-done | bytes 2080 | tf_op jit(solution)/shard_map/ppermute | solution.py:286
  70.0 7.2 %collective-permute-start.11 = (f32[4,128]{1,0:T(4,128)S(1)}, f32[4,128]{1,0:T(4,128)S(1)}, u32[]{:S(2)}, u32[]{:S(2)}) collective-permute-start(f32[4,128]{1,0:T(4,128)S(1)} %add.147), channel_id=1, source_target_pairs={{0,8},{1,9},{2,10},{3,11},{4,12},{5,13},{6,14},{7,15},{8,0},{9,1},... | collective-permute-start | bytes 6152 | tf_op jit(solution)/shard_map/ppermute | solution.py:286
  77.3 0.1 reshape.56
  77.4 0.7 copy.23
  78.1 1.0 %broadcast_in_dim_reshape.6 = bf16[1,1,256,2,512]{4,3,2,1,0:T(2,128)(2,1)} reshape(bf16[256,2,4,128]{3,2,1,0:T(4,128)(2,1)S(1)} %copy.23) | data formatting | bytes 1048576 | tf_op jit(solution)/shard_map/broadcast_in_dim;reshape | solution.py:322
  79.1 0.6 multiply_bitcast_fusion
  79.7 0.1 reduce
  79.9 0.3 copy.24
  80.3 0.8 broadcast_in_dim_reshape.7
  (60 shorter events, 0.8 us)
Async XLA Ops:
  0.6 1.6 %copy-start.12 = (f32[512]{0:T(512)S(1)}, f32[512]{0:T(512)}, u32[]{:S(2)}) copy-start(f32[512]{0:T(512)} %param.10) | copy-start | bytes 6148
  0.6 6.0 %copy-start.9 = (bf16[1,1,256,2560]{3,2,1,0:T(8,128)(2,1)S(1)}, bf16[1,1,256,2560]{3,2,1,0:T(8,128)(2,1)}, u32[]{:S(2)}) copy-start(bf16[1,1,256,2560]{3,2,1,0:T(8,128)(2,1)} %param.13) | copy-start | bytes 3932164
  2.2 7.8 %copy-start.10 = (bf16[1,1,256,2,512]{4,3,2,1,0:T(2,128)(2,1)S(1)}, bf16[1,1,256,2,512]{4,3,2,1,0:T(2,128)(2,1)}, u32[]{:S(2)}) copy-start(bf16[1,1,256,2,512]{4,3,2,1,0:T(2,128)(2,1)} %param.8) | copy-start | bytes 1572868
  2.3 22.4 %copy-start.1 = (bf16[4,128,256]{2,1,0:T(8,128)(2,1)}, bf16[4,128,256]{2,1,0:T(8,128)(2,1)S(1)}, u32[]{:S(2)}) copy-start(bf16[4,128,256]{2,1,0:T(8,128)(2,1)S(1)} %maximum_bitcast_fusion.1.refs_0_) | copy-start | bytes 786436
  2.3 8.6 %collective-permute-start.2 = (bf16[4,128,256]{2,1,0:T(8,128)(2,1)S(1)}, bf16[4,128,256]{2,1,0:T(8,128)(2,1)S(1)}, u32[]{:S(2)}, u32[]{:S(2)}) collective-permute-start(bf16[4,128,256]{2,1,0:T(8,128)(2,1)S(1)} %maximum_bitcast_fusion.1.refs_0_), channel_id=1, source_target_pairs={{0,96},{32,0},{64,32},{96,64},{128,224},{160,128},{192,160},{224,1... | collective-permute-start | bytes 786440 | tf_op jit(solution)/shard_map/ppermute | solution.py:266
  4.7 20.0 %collective-permute-start.1 = (bf16[4,128,256]{2,1,0:T(8,128)(2,1)S(1)}, bf16[4,128,256]{2,1,0:T(8,128)(2,1)S(1)}, u32[]{:S(2)}, u32[]{:S(2)}) collective-permute-start(bf16[4,128,256]{2,1,0:T(8,128)(2,1)S(1)} %maximum_bitcast_fusion.1.refs_0_), channel_id=1, source_target_pairs={{0,32},{32,64},{64,96},{96,0},{128,160},{160,192},{192,224},{224,1... | collective-permute-start | bytes 786440 | tf_op jit(solution)/shard_map/ppermute | solution.py:266
  4.7 8.4 %collective-permute-start = (bf16[4,128,256]{2,1,0:T(8,128)(2,1)S(1)}, bf16[4,128,256]{2,1,0:T(8,128)(2,1)S(1)}, u32[]{:S(2)}, u32[]{:S(2)}) collective-permute-start(bf16[4,128,256]{2,1,0:T(8,128)(2,1)S(1)} %maximum_bitcast_fusion.1.refs_0_), channel_id=1, source_target_pairs={{0,128},{32,160},{64,192},{96,224},{128,0},{160,32},{192,64},{224,... | collective-permute-start | bytes 786440 | tf_op jit(solution)/shard_map/ppermute | solution.py:266
  7.0 12.5 %collective-permute-start.7 = (f32[4,128]{1,0:T(4,128)S(1)}, f32[4,128]{1,0:T(4,128)S(1)}, u32[]{:S(2)}, u32[]{:S(2)}) collective-permute-start(f32[4,128]{1,0:T(4,128)S(1)} %reduce_sum.28), channel_id=1, source_target_pairs={{0,16},{1,17},{2,18},{3,19},{4,20},{5,21},{6,22},{7,23},{8,24},{9,... | collective-permute-start | bytes 6152 | tf_op jit(solution)/shard_map/ppermute | solution.py:286
  10.9 27.0 %copy-start.2 = (bf16[4,128,256]{2,1,0:T(8,128)(2,1)}, bf16[4,128,256]{2,1,0:T(8,128)(2,1)S(1)}, u32[]{:S(2)}) copy-start(bf16[4,128,256]{2,1,0:T(8,128)(2,1)S(1)} %collective-permute-done.2.refs_3_) | copy-start | bytes 786436
  11.0 7.0 %collective-permute-start.4 = (bf16[4,128,256]{2,1,0:T(8,128)(2,1)S(1)}, bf16[4,128,256]{2,1,0:T(8,128)(2,1)S(1)}, u32[]{:S(2)}, u32[]{:S(2)}) collective-permute-start(bf16[4,128,256]{2,1,0:T(8,128)(2,1)S(1)} %collective-permute-done.2.refs_3_), channel_id=1, source_target_pairs={{0,128},{32,160},{64,192},{96,224},{128,0},{160,32},{192,64},{224,... | collective-permute-start | bytes 786440 | tf_op jit(solution)/shard_map/ppermute | solution.py:266
  12.1 25.8 %copy-start = (bf16[4,256,256]{2,1,0:T(8,128)(2,1)}, bf16[4,256,256]{2,1,0:T(8,128)(2,1)S(1)}, u32[]{:S(2)}) copy-start(bf16[4,256,256]{2,1,0:T(8,128)(2,1)S(1)} %maximum_bitcast_fusion.kvr_ref) | copy-start | bytes 1572868
  12.1 12.5 %collective-permute-start.5 = (bf16[4,128,256]{2,1,0:T(8,128)(2,1)S(1)}, bf16[4,128,256]{2,1,0:T(8,128)(2,1)S(1)}, u32[]{:S(2)}, u32[]{:S(2)}) collective-permute-start(bf16[4,128,256]{2,1,0:T(8,128)(2,1)S(1)} %collective-permute-done.2.refs_3_), channel_id=1, source_target_pairs={{0,96},{32,0},{64,32},{96,64},{128,224},{160,128},{192,160},{224,1... | collective-permute-start | bytes 786440 | tf_op jit(solution)/shard_map/ppermute | solution.py:266
  13.0 24.9 %copy-start.4 = (bf16[4,128,256]{2,1,0:T(8,128)(2,1)}, bf16[4,128,256]{2,1,0:T(8,128)(2,1)S(1)}, u32[]{:S(2)}) copy-start(bf16[4,128,256]{2,1,0:T(8,128)(2,1)S(1)} %collective-permute-done.refs_1_) | copy-start | bytes 786436
  13.0 11.6 %collective-permute-start.3 = (bf16[4,128,256]{2,1,0:T(8,128)(2,1)S(1)}, bf16[4,128,256]{2,1,0:T(8,128)(2,1)S(1)}, u32[]{:S(2)}, u32[]{:S(2)}) collective-permute-start(bf16[4,128,256]{2,1,0:T(8,128)(2,1)S(1)} %collective-permute-done.refs_1_), channel_id=1, source_target_pairs={{0,32},{32,64},{64,96},{96,0},{128,160},{160,192},{192,224},{224,1... | collective-permute-start | bytes 786440 | tf_op jit(solution)/shard_map/ppermute | solution.py:266
  18.0 20.0 %copy-start.5 = (bf16[4,128,256]{2,1,0:T(8,128)(2,1)}, bf16[4,128,256]{2,1,0:T(8,128)(2,1)S(1)}, u32[]{:S(2)}) copy-start(bf16[4,128,256]{2,1,0:T(8,128)(2,1)S(1)} %collective-permute-done.4.refs_5_) | copy-start | bytes 786436
  18.0 6.8 %collective-permute-start.6 = (bf16[4,128,256]{2,1,0:T(8,128)(2,1)S(1)}, bf16[4,128,256]{2,1,0:T(8,128)(2,1)S(1)}, u32[]{:S(2)}, u32[]{:S(2)}) collective-permute-start(bf16[4,128,256]{2,1,0:T(8,128)(2,1)S(1)} %collective-permute-done.4.refs_5_), channel_id=1, source_target_pairs={{0,96},{32,0},{64,32},{96,64},{128,224},{160,128},{192,160},{224,1... | collective-permute-start | bytes 786440 | tf_op jit(solution)/shard_map/ppermute | solution.py:266
  19.5 5.1 %collective-permute-start.8 = (f32[4,128]{1,0:T(4,128)S(1)}, f32[4,128]{1,0:T(4,128)S(1)}, u32[]{:S(2)}, u32[]{:S(2)}) collective-permute-start(f32[4,128]{1,0:T(4,128)S(1)} %add_add_fusion), channel_id=1, source_target_pairs={{0,4},{1,5},{2,6},{3,7},{4,0},{5,1},{6,2},{7,3},{8,12},{9,13},{10,... | collective-permute-start | bytes 6152 | tf_op jit(solution)/shard_map/ppermute | solution.py:286
  24.6 13.3 %copy-start.3 = (bf16[4,128,256]{2,1,0:T(8,128)(2,1)}, bf16[4,128,256]{2,1,0:T(8,128)(2,1)S(1)}, u32[]{:S(2)}) copy-start(bf16[4,128,256]{2,1,0:T(8,128)(2,1)S(1)} %collective-permute-done.1.refs_2_) | copy-start | bytes 786436
  24.7 13.3 %copy-start.6 = (bf16[4,128,256]{2,1,0:T(8,128)(2,1)}, bf16[4,128,256]{2,1,0:T(8,128)(2,1)S(1)}, u32[]{:S(2)}) copy-start(bf16[4,128,256]{2,1,0:T(8,128)(2,1)S(1)} %collective-permute-done.5.refs_6_) | copy-start | bytes 786436
  24.7 13.3 %copy-start.7 = (bf16[4,128,256]{2,1,0:T(8,128)(2,1)}, bf16[4,128,256]{2,1,0:T(8,128)(2,1)S(1)}, u32[]{:S(2)}) copy-start(bf16[4,128,256]{2,1,0:T(8,128)(2,1)S(1)} %collective-permute-done.3.refs_4_) | copy-start | bytes 786436
  24.7 13.3 %copy-start.8 = (bf16[4,128,256]{2,1,0:T(8,128)(2,1)}, bf16[4,128,256]{2,1,0:T(8,128)(2,1)S(1)}, u32[]{:S(2)}) copy-start(bf16[4,128,256]{2,1,0:T(8,128)(2,1)S(1)} %collective-permute-done.6.refs_7_) | copy-start | bytes 786436
  38.0 20.6 %all-to-all-start = ((bf16[8,272,256]{2,1,0:T(8,128)(2,1)}), bf16[8,272,256]{2,1,0:T(8,128)(2,1)S(1)}, u32[]{:S(2)}, u32[]{:S(2)}) async-start(bf16[8,272,256]{2,1,0:T(8,128)(2,1)} %get-tuple-element.22), calls=%async_computation | async-start | bytes 2228224 | tf_op jit(solution)/shard_map/all_to_all | solution.py:310
  59.4 5.8 %copy-start.13 = (f32[4,128]{1,0:T(4,128)S(1)}, f32[4,128]{1,0:T(4,128)}, u32[]{:S(2)}) copy-start(f32[4,128]{1,0:T(4,128)} %get-tuple-element.26) | copy-start | bytes 6148
  59.4 20.3 %all-to-all-start.1 = ((bf16[8,256,256]{2,1,0:T(8,128)(2,1)}), bf16[8,256,256]{2,1,0:T(8,128)(2,1)S(1)}, u32[]{:S(2)}, u32[]{:S(2)}) async-start(bf16[8,256,256]{2,1,0:T(8,128)(2,1)} %get-tuple-element.25), calls=%async_computation.1 | async-start | bytes 2097152 | tf_op jit(solution)/shard_map/all_to_all | solution.py:313
  65.3 1.2 %collective-permute-start.9 = (f32[4,128]{1,0:T(4,128)S(1)}, f32[4,128]{1,0:T(4,128)S(1)}, u32[]{:S(2)}, u32[]{:S(2)}) collective-permute-start(f32[4,128]{1,0:T(4,128)S(1)} %copy-done.13), channel_id=1, source_target_pairs={{0,1},{1,0},{2,3},{3,2},{4,5},{5,4},{6,7},{7,6},{8,9},{9,8},{10,11... | collective-permute-start | bytes 6152 | tf_op jit(solution)/shard_map/ppermute | solution.py:286
  66.4 3.6 %collective-permute-start.10 = (f32[4,128]{1,0:T(4,128)S(1)}, f32[4,128]{1,0:T(4,128)S(1)}, u32[]{:S(2)}, u32[]{:S(2)}) collective-permute-start(f32[4,128]{1,0:T(4,128)S(1)} %add.146), channel_id=1, source_target_pairs={{0,2},{1,3},{2,0},{3,1},{4,6},{5,7},{6,4},{7,5},{8,10},{9,11},{10,... | collective-permute-start | bytes 6152 | tf_op jit(solution)/shard_map/ppermute | solution.py:286
  70.0 9.1 %collective-permute-start.11 = (f32[4,128]{1,0:T(4,128)S(1)}, f32[4,128]{1,0:T(4,128)S(1)}, u32[]{:S(2)}, u32[]{:S(2)}) collective-permute-start(f32[4,128]{1,0:T(4,128)S(1)} %add.147), channel_id=1, source_target_pairs={{0,8},{1,9},{2,10},{3,11},{4,12},{5,13},{6,14},{7,15},{8,0},{9,1},... | collective-permute-start | bytes 6152 | tf_op jit(solution)/shard_map/ppermute | solution.py:286
  77.4 1.7 %copy-start.11 = (f32[256,256]{1,0:T(8,128)S(1)}, f32[256,256]{1,0:T(8,128)}, u32[]{:S(2)}) copy-start(f32[256,256]{1,0:T(8,128)} %get-tuple-element.24) | copy-start | bytes 786436
